TPU v7x, 256 devices: a whole 4x4x8 slice. The times are simulated.
256 devices in a mesh: row: 4 (over x_hi, core), col: 64 (over z, y, x_lo).
Axes of the slice: x: 4 (x_hi: 2, x_lo: 2; x = x_hi * 2 + x_lo), y: 4, z: 8, core: 2. Of those that a mesh axis runs over, the one named last changes fastest.
Arguments:
- green_vectors: float32 [512, 131072], P('row', 'col'), may hold values from -6 to 6
- amplitudes: float32 [2048, 131072], P('row', 'col'), may hold values from -0.015625 to 0.015625
- cholesky: float32 [2048, 4096], P(('row', 'col')), may hold values from -0.125 to 0.125
Outputs:
- force_bias: float32 [512, 4096], P('col', 'row')
All inputs are finite; a program needn't handle non-finite values.
Results may differ from a plain program's by a relative error of at most 0.000084.
Values sent between devices are 32-bit elements; how exact they have to be, the bound alone decides.
No kernel may reach another device: no remote copies, remote signals or barrier semaphores. Data moves between devices by JAX's collectives and lax.ppermute only.
A program may use at most 64 MiB of HBM per device.

v0:
```python
import jax
import jax.numpy as jnp
from jax import lax
from jax.sharding import PartitionSpec as P


def per_device(green_vectors, amplitudes, cholesky):
    partial_terms = lax.dot_general(
        lax.all_gather(green_vectors, "row", axis=0, tiled=True),
        amplitudes,
        (((1,), (1,)), ((), ())),
        precision=lax.Precision.HIGHEST,
        preferred_element_type=jnp.float32,
    )
    local_walkers = lax.psum_scatter(partial_terms, "col", scatter_dimension=0, tiled=True)
    row_terms = jnp.dot(
        local_walkers,
        lax.all_gather(cholesky, "col", axis=0, tiled=True),
        precision=lax.Precision.HIGHEST,
        preferred_element_type=jnp.float32,
    )
    return lax.psum_scatter(row_terms, "row", scatter_dimension=1, tiled=True)


def solution(mesh):
    placed = (P("row", "col"), P("row", "col"), P(("row", "col"), None))
    return jax.shard_map(
        per_device, mesh=mesh, in_specs=placed, out_specs=P("col", "row"), check_vma=False
    )
```

profile of v0, /device:TPU:1, one launch (start us, length us, event | category | flops | bytes accessed | tf_op | source)
XLA Modules:
  0.0 734.7 jit_solution(10941447611964940108)
XLA Ops:
  6.5 0.0 all-gather.3.cloned.1.call-start
  6.5 0.7 all-gather.3.cloned.1.call-update
  7.3 0.0 reduce-scatter.3.cloned.1.call-start
  7.3 47.2 %all-gather.3.cloned.1.call-done = f32[512,2048]{1,0:T(8,128)} async-done(((f32[128,2048]{1,0:T(8,128)}), f32[512,2048]{1,0:T(8,128)}) %all-gather.3.cloned.1.call-update) | async-done | bytes 4194320 | tf_op jit(solution)/shard_map/all_gather | solution.py:9
  54.5 10.3 %fusion = f32[512,512]{1,0:T(8,128)} fusion(f32[512,2048]{1,0:T(8,128)} %all-gather.3.cloned.1.call-done, f32[512,2048]{1,0:T(8,128)} %param.4), kind=kOutput, calls=%fused_computation | convolution fusion | flops 6442450944 | bytes 9437184 | tf_op jit(solution)/shard_map/dot_general | solution.py:8
  64.8 0.0 reduce-scatter.3.cloned.1.call-update
  64.8 0.0 all-gather.5.cloned.1.call-start
  64.9 0.7 all-gather.5.cloned.1.call-update
  65.6 0.0 reduce-scatter.5.cloned.1.call-start
  65.6 261.9 %reduce-scatter.3.cloned.1.call-done = f32[8,512]{1,0:T(8,128)} async-done(((f32[512,512]{1,0:T(8,128)}), f32[8,512]{1,0:T(8,128)}) %reduce-scatter.3.cloned.1.call-update) | async-done | bytes 16400 | tf_op jit(solution)/shard_map/reduce_scatter | solution.py:15
  327.5 324.7 %all-gather.5.cloned.1.call-done = f32[512,4096]{1,0:T(8,128)} async-done(((f32[8,4096]{1,0:T(8,128)}), f32[512,4096]{1,0:T(8,128)}) %all-gather.5.cloned.1.call-update) | async-done | bytes 8388624 | tf_op jit(solution)/shard_map/all_gather | solution.py:18
  652.2 8.1 %fusion.1 = f32[8,4096]{1,0:T(8,128)} fusion(f32[8,512]{1,0:T(8,128)} %reduce-scatter.3.cloned.1.call-done, f32[512,4096]{1,0:T(8,128)} %all-gather.5.cloned.1.call-done), kind=kOutput, calls=%fused_computation.1 | convolution fusion | flops 201326592 | bytes 8536064 | tf_op jit(solution)/shard_map/dot_general | solution.py:16
  660.3 0.0 reduce-scatter.5.cloned.1.call-update
  660.3 67.9 %reduce-scatter.5.cloned.1.call-done = f32[8,1024]{1,0:T(8,128)} async-done(((f32[8,4096]{1,0:T(8,128)}), f32[8,1024]{1,0:T(8,128)}) %reduce-scatter.5.cloned.1.call-update) | async-done | bytes 32784 | tf_op jit(solution)/shard_map/reduce_scatter | solution.py:22
Async XLA Ops:
  6.5 47.9 %all-gather.3.cloned.1.call-start = ((), (), s32[]{:S(2)}) async-start(), calls=%async_computation.2 | async-start | bytes 5242880 | tf_op jit(solution)/shard_map/all_gather | solution.py:9
  7.3 320.2 %reduce-scatter.3.cloned.1.call-start = ((), (), s32[]{:S(2)}) async-start(), calls=%async_computation.3 | async-start | bytes 1064960 | tf_op jit(solution)/shard_map/reduce_scatter | solution.py:15
  64.8 587.4 %all-gather.5.cloned.1.call-start = ((), (), s32[]{:S(2)}) async-start(), calls=%async_computation.4 | async-start | bytes 8519680 | tf_op jit(solution)/shard_map/all_gather | solution.py:18
  65.6 662.6 %reduce-scatter.5.cloned.1.call-start = ((), (), s32[]{:S(2)}) async-start(), calls=%async_computation.5 | async-start | bytes 163840 | tf_op jit(solution)/shard_map/reduce_scatter | solution.py:22
Sparse Core Ops, SparseCore 0:
  9.2 45.2 all-gather.2
  65.0 262.4 reduce-scatter.2
  329.4 322.7 all-gather.4
  660.4 67.7 reduce-scatter.4
where the time goes:
time: 735 us
  waiting for transfers between devices  703 us (96%)
  matrix products  18.4 us (3%)
  between operations  13.1 us (2%)
    all_gather x1, waiting for transfers between devices, per_device(): lax.all_gather(cholesky, 'col', axis=0, tiled=True)  325 us
    reduce_scatter x1, waiting for transfers between devices, per_device(): lax.psum_scatter(partial_terms, 'col', scatter_dimension=0, tiled=True)  262 us
    reduce_scatter x1, waiting for transfers between devices, per_device(): return lax.psum_scatter(row_terms, 'row', scatter_dimension=1, tiled=True)  67.9 us
    all_gather x1, waiting for transfers between devices, per_device(): lax.all_gather(green_vectors, 'row', axis=0, tiled=True)  47.2 us
  transfers between devices with their start and end apart: 4, of which 4 were waited for; matrix products, arithmetic and copies ran while one was open for 0% of the time, Pallas kernels for 0%

commit v1 on v0

v1 whole, which is shorter than its diff:
```python
import itertools

import jax
import jax.numpy as jnp
import numpy as np
from jax import lax
from jax.sharding import Mesh, PartitionSpec as P

SIZES = {"xh": 2, "c": 2, "zh": 4, "z0": 2, "yh": 2, "y0": 2, "xl": 2}
AXES = tuple(SIZES)
ROW = ("xh", "c")
COL = ("zh", "z0", "yh", "y0", "xl")
HIGH = lax.Precision.HIGH


def move(x, axis):
    return lax.ppermute(x, axis, [(0, 1), (1, 0)])


def exchange(pieces, axes):
    got = lax.all_to_all(pieces, axes, 0, 0, tiled=True)
    return jnp.sum(got, axis=0)


def partial_terms(green, amplitudes):
    walkers = green.reshape(256, -1)
    terms = lax.dot_general(
        walkers, amplitudes, (((1,), (1,)), ((), ())), precision=HIGH, preferred_element_type=jnp.float32
    )
    terms = terms.reshape(2, 4, 32, 4, 128).transpose(1, 3, 0, 2, 4).reshape(16, 64, 128)
    return exchange(terms, ("z0", "yh", "y0", "xl")).reshape(2, 32, 128)


def per_device(green, amplitudes, cholesky):
    green_x = move(green, "xh")
    green_c = move(green, "c")
    factors = lax.all_gather(cholesky, ("zh", "z0", "yh"), axis=0, tiled=True)

    amplitudes = amplitudes.reshape(16, 4, 8, -1).transpose(1, 0, 2, 3).reshape(512, -1)
    near = partial_terms(jnp.stack([green, green_c]), amplitudes)
    green_xc = move(green_x, "c")
    far = partial_terms(jnp.stack([green_x, green_xc]), amplitudes)

    blocks = jnp.concatenate([near, far])
    blocks = jnp.where(lax.axis_index("xh") == 1, jnp.concatenate([far, near]), blocks)
    swapped = jnp.stack([blocks[1], blocks[0], blocks[3], blocks[2]])
    blocks = jnp.where(lax.axis_index("c") == 1, swapped, blocks)
    effective = exchange(blocks, ("zh",))

    bias = jnp.dot(effective, factors, precision=HIGH, preferred_element_type=jnp.float32)
    bias = bias.reshape(4, 8, 4, 1024).transpose(2, 0, 1, 3).reshape(16, 8, 1024)
    return exchange(bias, ("xh", "c", "y0", "xl"))


def solution(mesh):
    parts = Mesh(mesh.devices.reshape(tuple(SIZES.values())), AXES)
    return jax.shard_map(
        per_device,
        mesh=parts,
        in_specs=(P(ROW, COL), P(ROW, COL), P(AXES, None)),
        out_specs=P(COL, ROW),
        check_vma=False,
    )
```

time: 735 us -> 130 us (0.18)
  waiting for transfers between devices: 703 us -> 52.2 us
  blocking collectives: 0 us -> 33.1 us
  starting transfers between devices: 0.12 us -> 17.2 us
  matrix products: 18.4 us -> 9.34 us
    all_gather x2 -> x1, waiting for transfers between devices: 372 us -> 15.8 us  [per_device(): factors = lax.all_gather(cholesky, ('zh', 'z0', 'yh'), axis=0, tiled=True)]
    reduce_scatter x2 -> x0, waiting for transfers between devices: 330 us -> none  [the longest x1 262 us: per_device(): lax.psum_scatter(partial_terms, 'col', scatter_dimension=0, tiled=True)]
    all_to_all x0 -> x2, blocking collectives: none -> 33.1 us  [exchange(): got = lax.all_to_all(pieces, axes, 0, 0, tiled=True)]
    ppermute x0 -> x3, waiting for transfers between devices: none -> 21.2 us  [move(): return lax.ppermute(x, axis, [(0, 1), (1, 0)])]
    all_to_all x0 -> x2, waiting for transfers between devices: none -> 15.3 us  [exchange(): got = lax.all_to_all(pieces, axes, 0, 0, tiled=True)]
    all_to_all x0 -> x2, starting transfers between devices: none -> 10.5 us  [exchange(): got = lax.all_to_all(pieces, axes, 0, 0, tiled=True)]
    dot_general x2 -> x3, matrix products: 18.4 us -> 9.34 us  [the longest x2 8.21 us: partial_terms(): lax.dot_general(walkers, amplitudes, (((1,), (1,)), ((), ())), precision=...]
  transfers between devices with their start and end apart: 4 -> 6, of which waited for: 4 -> 4; matrix products, arithmetic and copies ran while one was open for 0% -> 8% of each run, Pallas kernels for 0% -> 0%
where the time goes in v1:
time: 130 us
  waiting for transfers between devices  52.2 us (40%)
  blocking collectives  33.1 us (25%)
  starting transfers between devices  17.2 us (13%)
  between operations  13.5 us (10%)
  matrix products  9.34 us (7%)
  local copies, waits for them, and re-layouts  3.62 us (3%)
    all_to_all x2, blocking collectives, exchange(): got = lax.all_to_all(pieces, axes, 0, 0, tiled=True)  33.1 us
    ppermute x3, waiting for transfers between devices, move(): return lax.ppermute(x, axis, [(0, 1), (1, 0)])  21.2 us
    all_gather x1, waiting for transfers between devices, per_device(): factors = lax.all_gather(cholesky, ('zh', 'z0', 'yh'), axis=0, tiled=True)  15.8 us
    all_to_all x2, waiting for transfers between devices, exchange(): got = lax.all_to_all(pieces, axes, 0, 0, tiled=True)  15.3 us
    all_to_all x2, starting transfers between devices, exchange(): got = lax.all_to_all(pieces, axes, 0, 0, tiled=True)  10.5 us
    dot_general x2, matrix products, partial_terms(): lax.dot_general(walkers, amplitudes, (((1,), (1,)), ((), ())), precision=...  8.21 us
    ppermute x3, starting transfers between devices, move(): return lax.ppermute(x, axis, [(0, 1), (1, 0)])  6.71 us
  transfers between devices with their start and end apart: 6, of which 4 were waited for; matrix products, arithmetic and copies ran while one was open for 8% of the time, Pallas kernels for 0%

profile of v1, /device:TPU:1, one launch (start us, length us, event | category | flops | bytes accessed | tf_op | source)
XLA Modules:
  0.0 129.7 jit_solution(17052103372337315445)
XLA Ops:
  6.5 0.0 all-gather.2.cloned.1.call-start
  6.5 3.6 %collective-permute-start = (f32[128,2048]{1,0:T(8,128)}, f32[128,2048]{1,0:T(8,128)S(1)}, u32[]{:S(2)}, u32[]{:S(2)}) collective-permute-start(f32[128,2048]{1,0:T(8,128)} %param.3), channel_id=1, source_target_pairs={{0,128},{128,0},{1,129},{129,1},{2,130},{130,2},{3,131},{131,3},{4... | collective-permute-start | bytes 3145736 | tf_op jit(solution)/shard_map/ppermute | solution.py:17
  10.1 1.0 collective-permute-start.2
  11.1 0.0 all-gather.2.cloned.1.call-update
  11.1 21.2 %collective-permute-done = f32[128,2048]{1,0:T(8,128)S(1)} collective-permute-done((f32[128,2048]{1,0:T(8,128)}, f32[128,2048]{1,0:T(8,128)S(1)}, u32[]{:S(2)}, u32[]{:S(2)}) %collective-permute-start) | collective-permute-done | bytes 1048608 | tf_op jit(solution)/shard_map/ppermute | solution.py:17
  32.3 2.2 %collective-permute-start.1 = (f32[128,2048]{1,0:T(8,128)S(1)}, f32[128,2048]{1,0:T(8,128)}, u32[]{:S(2)}, u32[]{:S(2)}) collective-permute-start(f32[128,2048]{1,0:T(8,128)S(1)} %collective-permute-done), channel_id=1, source_target_pairs={{0,64},{64,0},{1,65},{65,1},{2,66},{66,2},{3,67},{67,3},{4,68},{68... | collective-permute-start | bytes 3145736 | tf_op jit(solution)/shard_map/ppermute | solution.py:17
  34.4 0.0 collective-permute-done.2
  34.4 4.1 %fusion.13 = f32[4,4,2,32,128]{4,3,1,0,2:T(8,128)S(1)} fusion(f32[4,16,8,2048]{3,2,0,1:T(8,128)} %bitcast.57, f32[1,4,32,2048]{3,2,1,0:T(8,128)S(1)} %bitcast.64, f32[1,4,32,2048]{3,2,1,0:T(8,128)} %bitcast.62), kind=kOutput, calls=%fused_computation.13 | convolution fusion | flops 1611137024 | bytes 6815744 | tf_op jit(solution)/shard_map/dot_general | solution.py:27
  38.5 0.8 copy.13
  39.4 6.8 %all-to-all-start.1 = ((f32[16,64,128]{2,1,0:T(8,128)}), f32[16,64,128]{2,1,0:T(8,128)S(1)}, u32[]{:S(2)}, u32[]{:S(2)}) async-start(f32[16,64,128]{2,1,0:T(8,128)} %bitcast.19), calls=%async_computation.1 | async-start | bytes 1048576 | tf_op jit(solution)/shard_map/all_to_all | solution.py:21
  46.2 0.0 collective-permute-done.1
  46.2 4.1 %fusion.10 = f32[4,4,2,32,128]{4,3,1,0,2:T(8,128)S(1)} fusion(f32[4,16,8,2048]{3,2,0,1:T(8,128)} %bitcast.58, f32[1,4,32,2048]{3,2,1,0:T(8,128)} %bitcast.1, f32[1,4,32,2048]{3,2,1,0:T(8,128)S(1)} %bitcast.63), kind=kOutput, calls=%fused_computation.12 | convolution fusion | flops 1611137024 | bytes 6815744 | tf_op jit(solution)/shard_map/dot_general | solution.py:27
  50.3 0.8 copy.12
  51.2 5.4 %all-to-all-done.1 = f32[16,64,128]{2,1,0:T(8,128)S(1)} async-done(((f32[16,64,128]{2,1,0:T(8,128)}), f32[16,64,128]{2,1,0:T(8,128)S(1)}, u32[]{:S(2)}, u32[]{:S(2)}) %all-to-all-start.1) | async-done | bytes 524320 | tf_op jit(solution)/shard_map/all_to_all | solution.py:21
  56.5 3.7 %all-to-all-start = ((f32[16,64,128]{2,1,0:T(8,128)}), f32[16,64,128]{2,1,0:T(8,128)S(1)}, u32[]{:S(2)}, u32[]{:S(2)}) async-start(f32[16,64,128]{2,1,0:T(8,128)} %bitcast.10), calls=%async_computation | async-start | bytes 1048576 | tf_op jit(solution)/shard_map/all_to_all | solution.py:21
  60.3 9.9 %all-to-all-done = f32[16,64,128]{2,1,0:T(8,128)S(1)} async-done(((f32[16,64,128]{2,1,0:T(8,128)}), f32[16,64,128]{2,1,0:T(8,128)S(1)}, u32[]{:S(2)}, u32[]{:S(2)}) %all-to-all-start) | async-done | bytes 524320 | tf_op jit(solution)/shard_map/all_to_all | solution.py:21
  70.3 15.0 %all_to_all.20 = f32[4,32,128]{2,1,0:T(8,128)S(1)} all-to-all(f32[4,32,128]{2,1,0:T(8,128)S(1)} %maximum_select_fusion.1), channel_id=1, replica_groups=mesh['xh'=2,'c'=2,'zh'=4,'z0'=2,'yh'=2,'y0'=2,'xl'=2] {'zh'}, dimensions={0} | all-to-all | bytes 131072 | tf_op jit(solution)/shard_map/all_to_all | solution.py:21
  85.3 15.8 %all-gather.2.cloned.1.call-done = f32[128,4096]{1,0:T(8,128)} async-done(((f32[8,4096]{1,0:T(8,128)}), f32[128,4096]{1,0:T(8,128)}) %all-gather.2.cloned.1.call-update) | async-done | bytes 2097168 | tf_op jit(solution)/shard_map/all_gather | solution.py:37
  101.0 1.9 %copy.14 = f32[4096,128]{1,0:T(8,128)S(1)} copy(f32[4096,128]{0,1:T(8,128)} %bitcast.60) | data formatting | bytes 4194304 | tf_op jit(solution)/shard_map/dot_general | solution.py:50
  102.9 1.1 convolution_bitcast_fusion
  104.1 18.1 %all_to_all.21 = f32[16,8,1024]{2,1,0:T(8,128)S(1)} all-to-all(f32[16,8,1024]{2,1,0:T(8,128)S(1)} %bitcast.61), channel_id=1, replica_groups=mesh['xh'=2,'c'=2,'zh'=4,'z0'=2,'yh'=2,'y0'=2,'xl'=2] {'xh','c','y0','xl'}, dimensions={0} | all-to-all | bytes 1048576 | tf_op jit(solution)/shard_map/all_to_all | solution.py:21
  122.2 0.6 reduce_sum.39
  (7 shorter events, 0.1 us)
Async XLA Ops:
  6.5 94.5 %all-gather.2.cloned.1.call-start = ((), (), s32[]{:S(2)}) async-start(), calls=%async_computation.4 | async-start | bytes 2228224 | tf_op jit(solution)/shard_map/all_gather | solution.py:37
  6.5 25.7 %collective-permute-start = (f32[128,2048]{1,0:T(8,128)}, f32[128,2048]{1,0:T(8,128)S(1)}, u32[]{:S(2)}, u32[]{:S(2)}) collective-permute-start(f32[128,2048]{1,0:T(8,128)} %param.3), channel_id=1, source_target_pairs={{0,128},{128,0},{1,129},{129,1},{2,130},{130,2},{3,131},{131,3},{4... | collective-permute-start | bytes 3145736 | tf_op jit(solution)/shard_map/ppermute | solution.py:17
  10.1 24.3 %collective-permute-start.2 = (f32[128,2048]{1,0:T(8,128)}, f32[128,2048]{1,0:T(8,128)S(1)}, u32[]{:S(2)}, u32[]{:S(2)}) collective-permute-start(f32[128,2048]{1,0:T(8,128)} %param.3), channel_id=1, source_target_pairs={{0,64},{64,0},{1,65},{65,1},{2,66},{66,2},{3,67},{67,3},{4,68},{68... | collective-permute-start | bytes 3145736 | tf_op jit(solution)/shard_map/ppermute | solution.py:17
  32.3 13.9 %collective-permute-start.1 = (f32[128,2048]{1,0:T(8,128)S(1)}, f32[128,2048]{1,0:T(8,128)}, u32[]{:S(2)}, u32[]{:S(2)}) collective-permute-start(f32[128,2048]{1,0:T(8,128)S(1)} %collective-permute-done), channel_id=1, source_target_pairs={{0,64},{64,0},{1,65},{65,1},{2,66},{66,2},{3,67},{67,3},{4,68},{68... | collective-permute-start | bytes 3145736 | tf_op jit(solution)/shard_map/ppermute | solution.py:17
  39.4 17.2 %all-to-all-start.1 = ((f32[16,64,128]{2,1,0:T(8,128)}), f32[16,64,128]{2,1,0:T(8,128)S(1)}, u32[]{:S(2)}, u32[]{:S(2)}) async-start(f32[16,64,128]{2,1,0:T(8,128)} %bitcast.19), calls=%async_computation.1 | async-start | bytes 1048576 | tf_op jit(solution)/shard_map/all_to_all | solution.py:21
  56.5 13.7 %all-to-all-start = ((f32[16,64,128]{2,1,0:T(8,128)}), f32[16,64,128]{2,1,0:T(8,128)S(1)}, u32[]{:S(2)}, u32[]{:S(2)}) async-start(f32[16,64,128]{2,1,0:T(8,128)} %bitcast.10), calls=%async_computation | async-start | bytes 1048576 | tf_op jit(solution)/shard_map/all_to_all | solution.py:21
Sparse Core Ops, SparseCore 0:
  11.2 89.7 all-gather.1

commit v2 on v1

v2 whole, which is shorter than its diff:
```python
import functools

import jax
import jax.numpy as jnp
from jax import lax
from jax.experimental import pallas as pl
from jax.experimental.pallas import tpu as pltpu
from jax.sharding import Mesh, PartitionSpec as P

SIZES = {"xh": 2, "c": 2, "z2": 2, "z1": 2, "z0": 2, "yh": 2, "y0": 2, "xl": 2}
AXES = tuple(SIZES)
ROW = ("xh", "c")
COL = ("z2", "z1", "z0", "yh", "y0", "xl")
VMEM_BYTES = 20 * 2**20
ALL_VMEM_BYTES = 56 * 2**20


def move(x, axis):
    return lax.ppermute(x, axis, [(0, 1), (1, 0)])


def in_order(x, other, axis):
    return jnp.where(lax.axis_index(axis) == 1, jnp.concatenate([other, x]), jnp.concatenate([x, other]))


def exchange(pieces, axes):
    return lax.all_to_all(pieces, axes, 0, 0, tiled=True)


def halves(x):
    high = x.astype(jnp.bfloat16)
    return high, (x - high.astype(jnp.float32)).astype(jnp.bfloat16)


def dot(x, y, contract):
    return lax.dot_general(x, y, (contract, ((), ())), preferred_element_type=jnp.float32)


def split_walkers(refs, walkers_ref):
    for block, ref in enumerate(refs):
        high, low = halves(ref[...])
        walkers_ref[128 * block : 128 * block + 128] = high
        walkers_ref[256 + 128 * block : 384 + 128 * block] = low


def write_terms(walkers_ref, high, low, out_ref):
    both = dot(walkers_ref[...], high, ((1,), (1,)))
    terms = both[:256] + (both[256:] + dot(walkers_ref[:256], low, ((1,), (1,))))
    for y in range(4):
        for run in range(4):
            out_ref[0, y, 16 * run : 16 * run + 16] = terms[64 * run + 16 * y : 64 * run + 16 * y + 16]


def near_kernel(green_ref, green_c_ref, amplitudes_ref, out_ref, high_ref, low_ref, walkers_ref):
    @pl.when(pl.program_id(0) == 0)
    def _():
        split_walkers((green_ref, green_c_ref), walkers_ref)

    for xl in range(2):
        for y in range(4):
            for zh in range(0, 4, 2):
                rows = jnp.concatenate([amplitudes_ref[zh, 0, y, xl], amplitudes_ref[zh + 1, 0, y, xl]])
                high, low = halves(rows)
                start = 128 * xl + 32 * y + 8 * zh
                high_ref[start : start + 16] = high
                low_ref[start : start + 16] = low
    write_terms(walkers_ref, high_ref[...], low_ref[...], out_ref)


def far_kernel(green_x_ref, green_xc_ref, high_ref, low_ref, out_ref, walkers_ref):
    @pl.when(pl.program_id(0) == 0)
    def _():
        split_walkers((green_x_ref, green_xc_ref), walkers_ref)

    write_terms(walkers_ref, high_ref[...], low_ref[...], out_ref)


def bias_kernel(effective_ref, factors_ref, out_ref):
    effective = halves(jnp.sum(effective_ref[...], axis=0))
    factors = halves(factors_ref[...])
    both = dot(jnp.concatenate(effective), factors[0], ((1,), (0,)))
    bias = both[:32] + (both[32:] + dot(effective[0], factors[1], ((1,), (0,))))
    out_ref[...] = bias.reshape(4, 8, 1024)


def near_terms(green, green_c, amplitudes):
    pairs = green.shape[1]
    walkers = pl.BlockSpec((128, pairs), lambda g: (0, 0))
    half = pl.BlockSpec((256, pairs), lambda g: (g, 0))
    halved = jax.ShapeDtypeStruct((512, pairs), jnp.bfloat16)
    return pl.pallas_call(
        near_kernel,
        out_shape=(jax.ShapeDtypeStruct((2, 4, 64, 256), jnp.float32), halved, halved),
        grid=(2,),
        in_specs=[walkers, walkers, pl.BlockSpec((4, 1, 4, 2, 8, pairs), lambda g: (0, g, 0, 0, 0, 0))],
        out_specs=(pl.BlockSpec((1, 4, 64, 256), lambda g: (g, 0, 0, 0)), half, half),
        scratch_shapes=[pltpu.VMEM((512, pairs), jnp.bfloat16)],
        compiler_params=pltpu.CompilerParams(vmem_limit_bytes=ALL_VMEM_BYTES),
        cost_estimate=pl.CostEstimate(flops=6 * 256 * 512 * pairs, bytes_accessed=11 * 2**20, transcendentals=0),
    )(green, green_c, amplitudes.reshape(4, 2, 4, 2, 8, pairs))


def far_terms(green_x, green_xc, high, low):
    pairs = green_x.shape[1]
    walkers = pl.BlockSpec((128, pairs), lambda g: (0, 0))
    half = pl.BlockSpec((256, pairs), lambda g: (g, 0))
    return pl.pallas_call(
        far_kernel,
        out_shape=jax.ShapeDtypeStruct((2, 4, 64, 256), jnp.float32),
        grid=(2,),
        in_specs=[walkers, walkers, half, half],
        out_specs=pl.BlockSpec((1, 4, 64, 256), lambda g: (g, 0, 0, 0)),
        scratch_shapes=[pltpu.VMEM((512, pairs), jnp.bfloat16)],
        compiler_params=pltpu.CompilerParams(vmem_limit_bytes=VMEM_BYTES),
        cost_estimate=pl.CostEstimate(flops=6 * 256 * 512 * pairs, bytes_accessed=6 * 2**20, transcendentals=0),
    )(green_x, green_xc, high, low)


def bias_terms(effective, factors):
    return pl.pallas_call(
        bias_kernel,
        out_shape=jax.ShapeDtypeStruct((16, 8, 1024), jnp.float32),
        grid=(4,),
        in_specs=[
            pl.BlockSpec((8, 32, 128), lambda g: (0, 0, 0)),
            pl.BlockSpec((128, 1024), lambda g: (0, g)),
        ],
        out_specs=pl.BlockSpec((4, 8, 1024), lambda g: (g, 0, 0)),
        compiler_params=pltpu.CompilerParams(vmem_limit_bytes=VMEM_BYTES),
        cost_estimate=pl.CostEstimate(flops=6 * 32 * 128 * 4096, bytes_accessed=3 * 2**20, transcendentals=0),
    )(effective, factors)


def per_device(green, amplitudes, cholesky):
    green_x = move(green, "xh")
    green_c = move(green, "c")
    other = move(cholesky, "z1")

    near, high, low = near_terms(green, green_c, amplitudes)
    near = exchange(near.reshape(8, 64, 256), ("z0", "yh", "y0"))
    high, other = lax.optimization_barrier((high, other))
    factors = in_order(cholesky, other, "z1")
    factors = in_order(factors, move(factors, "z2"), "z2")
    factors = lax.all_gather(factors, ("yh", "y0"), axis=0, tiled=True)

    near, green_x = lax.optimization_barrier((near, green_x))
    far = far_terms(green_x, move(green_x, "c"), high, low)
    far = exchange(far.reshape(8, 64, 256), ("z0", "yh", "y0"))

    near = jnp.sum(near, axis=0).reshape(2, 32, 2, 128)
    far = jnp.sum(far, axis=0).reshape(2, 32, 2, 128)
    blocks = jnp.concatenate([near, far])
    blocks = jnp.where(lax.axis_index("xh") == 1, jnp.concatenate([far, near]), blocks)
    swapped = jnp.stack([blocks[1], blocks[0], blocks[3], blocks[2]])
    blocks = jnp.where(lax.axis_index("c") == 1, swapped, blocks)
    effective = exchange(blocks.transpose(0, 2, 1, 3).reshape(8, 32, 128), ("z2", "z1", "xl"))

    bias = exchange(bias_terms(effective, factors), ("xh", "c", "z0", "xl"))
    return jnp.sum(bias, axis=0)


def solution(mesh):
    parts = Mesh(mesh.devices.reshape(tuple(SIZES.values())), AXES)
    return jax.shard_map(
        per_device,
        mesh=parts,
        in_specs=(P(ROW, COL), P(ROW, COL), P(AXES, None)),
        out_specs=P(COL, ROW),
        check_vma=False,
    )
```

time: 130 us -> 105 us (0.81)
  waiting for transfers between devices: 52.2 us -> 25 us
  Pallas kernels: 0 us -> 9.75 us
  matrix products: 9.34 us -> 0 us
  blocking collectives: 33.1 us -> 25.2 us
  starting transfers between devices: 17.2 us -> 23.3 us
  other arithmetic: 0.75 us -> 3.81 us
    ppermute x3 -> x5, waiting for transfers between devices: 21.2 us -> 6.05 us  [move(): return lax.ppermute(x, axis, [(0, 1), (1, 0)])]
    all_gather x1, waiting for transfers between devices: 15.8 us -> 1.18 us  [per_device(): factors = lax.all_gather(factors, ('yh', 'y0'), axis=0, tiled=True)]
    pallas_call x0 -> x3, Pallas kernels: none -> 9.75 us  [the longest x1 5.67 us: near_terms(): pl.pallas_call(near_kernel, out_shape=(jax.ShapeDtypeStruct((2, 4, 64, 25...]
    dot_general x3 -> x0, matrix products: 9.34 us -> none  [the longest x2 8.21 us: partial_terms(): lax.dot_general(walkers, amplitudes, (((1,), (1,)), ((), ())), precision=...]
    ppermute x3 -> x5, starting transfers between devices: 6.71 us -> 15.6 us  [move(): return lax.ppermute(x, axis, [(0, 1), (1, 0)])]
    all_to_all x2, blocking collectives: 33.1 us -> 25.2 us  [exchange(): return lax.all_to_all(pieces, axes, 0, 0, tiled=True)]
    unnamed x0 -> x10, local copies, waits for them, and re-layouts: none -> 4.15 us
    all_to_all x2, starting transfers between devices: 10.5 us -> 7.68 us  [exchange(): return lax.all_to_all(pieces, axes, 0, 0, tiled=True)]
  transfers between devices with their start and end apart: 6 -> 8, of which waited for: 4 -> 5; matrix products, arithmetic and copies ran while one was open for 8% -> 3% of each run, Pallas kernels for 0% -> 8%
where the time goes in v2:
time: 105 us
  blocking collectives  25.2 us (24%)
  waiting for transfers between devices  25 us (24%)
  starting transfers between devices  23.3 us (22%)
  between operations  13.5 us (13%)
  Pallas kernels  9.75 us (9%)
  local copies, waits for them, and re-layouts  4.24 us (4%)
  other arithmetic  3.81 us (4%)
    all_to_all x2, blocking collectives, exchange(): return lax.all_to_all(pieces, axes, 0, 0, tiled=True)  25.2 us
    all_to_all x2, waiting for transfers between devices, exchange(): return lax.all_to_all(pieces, axes, 0, 0, tiled=True)  17.8 us
    ppermute x5, starting transfers between devices, move(): return lax.ppermute(x, axis, [(0, 1), (1, 0)])  15.6 us
    all_to_all x2, starting transfers between devices, exchange(): return lax.all_to_all(pieces, axes, 0, 0, tiled=True)  7.68 us
    ppermute x5, waiting for transfers between devices, move(): return lax.ppermute(x, axis, [(0, 1), (1, 0)])  6.05 us
    pallas_call x1, Pallas kernels, near_terms(): pl.pallas_call(near_kernel, out_shape=(jax.ShapeDtypeStruct((2, 4, 64, 25...  5.67 us
    unnamed x10, local copies, waits for them, and re-layouts  4.15 us
    pallas_call x1, Pallas kernels, far_terms(): pl.pallas_call(far_kernel, out_shape=jax.ShapeDtypeStruct((2, 4, 64, 256)...  3.04 us
  transfers between devices with their start and end apart: 8, of which 5 were waited for; matrix products, arithmetic and copies ran while one was open for 3% of the time, Pallas kernels for 8%

profile of v2, /device:TPU:1, one launch (start us, length us, event | category | flops | bytes accessed | tf_op | source)
XLA Modules:
  0.0 104.8 jit_solution(18185311912600503965)
XLA Ops:
  6.5 3.2 %collective-permute-start = (f32[128,2048]{1,0:T(8,128)}, f32[128,2048]{1,0:T(8,128)S(1)}, u32[]{:S(2)}, u32[]{:S(2)}) collective-permute-start(f32[128,2048]{1,0:T(8,128)} %green_ref.1), channel_id=1, source_target_pairs={{0,64},{64,0},{1,65},{65,1},{2,66},{66,2},{3,67},{67,3},{4,68},{68... | collective-permute-start | bytes 3145736 | tf_op jit(solution)/shard_map/ppermute | solution.py:19
  9.8 1.0 collective-permute-start.1
  10.8 3.0 %collective-permute-start.3 = (f32[8,4096]{1,0:T(8,128)}, f32[8,4096]{1,0:T(8,128)S(1)}, u32[]{:S(2)}, u32[]{:S(2)}) collective-permute-start(f32[8,4096]{1,0:T(8,128)} %param.5), channel_id=1, source_target_pairs={{0,16},{16,0},{1,17},{17,1},{2,18},{18,2},{3,19},{19,3},{4,20},{20... | collective-permute-start | bytes 393224 | tf_op jit(solution)/shard_map/ppermute | solution.py:19
  13.8 1.0 copy-done.3
  14.7 5.7 %shard_map.37 = (f32[2,4,64,256]{3,2,1,0:T(8,128)}, bf16[512,2048]{1,0:T(8,128)(2,1)}, bf16[512,2048]{1,0:T(8,128)(2,1)}) custom-call(f32[128,2048]{1,0:T(8,128)} %green_ref.1, f32[128,2048]{1,0:T(8,128)} %copy-done.3, f32[4,2,4,2,8,2048]{5,4,3,2,1,0:T(8,128)} %bitcast.6), custom_call_target="tpu_custom_call" | custom-call | flops 1610612736 | bytes 11534336 | tf_op jit(solution)/shard_map/pallas_call | solution.py:91
  20.5 6.2 %collective-permute-start.4 = (f32[16,4096]{1,0:T(8,128)S(1)}, f32[16,4096]{1,0:T(8,128)}, u32[]{:S(2)}, u32[]{:S(2)}) collective-permute-start(f32[16,4096]{1,0:T(8,128)S(1)} %maximum_select_fusion.1), channel_id=1, source_target_pairs={{0,32},{32,0},{1,33},{33,1},{2,34},{34,2},{3,35},{35,3},{4,36},{36... | collective-permute-start | bytes 786440 | tf_op jit(solution)/shard_map/ppermute | solution.py:19
  26.7 4.2 %all-to-all-start = ((f32[8,64,256]{2,1,0:T(8,128)}), f32[8,64,256]{2,1,0:T(8,128)}, u32[]{:S(2)}, u32[]{:S(2)}) async-start(f32[8,64,256]{2,1,0:T(8,128)} %bitcast.7), calls=%async_computation | async-start | bytes 1048576 | tf_op jit(solution)/shard_map/all_to_all | solution.py:27
  31.0 3.7 %collective-permute-done.4 = f32[16,4096]{1,0:T(8,128)} collective-permute-done((f32[16,4096]{1,0:T(8,128)S(1)}, f32[16,4096]{1,0:T(8,128)}, u32[]{:S(2)}, u32[]{:S(2)}) %collective-permute-start.4) | collective-permute-done | bytes 262176 | tf_op jit(solution)/shard_map/ppermute | solution.py:19
  34.7 1.9 %maximum_select_fusion = f32[32,4096]{1,0:T(8,128)} fusion(f32[16,4096]{1,0:T(8,128)S(1)} %maximum_select_fusion.1, f32[16,4096]{1,0:T(8,128)} %collective-permute-done.4, pred[]{:T(512)S(6)} %eq.14), kind=kLoop, calls=%fused_computation | loop fusion | flops 393216 | bytes 1048577 | tf_op jit(solution)/shard_map/jit(_where)/select_n | solution.py:23
  36.6 8.0 %all-to-all-done = f32[8,64,256]{2,1,0:T(8,128)} async-done(((f32[8,64,256]{2,1,0:T(8,128)}), f32[8,64,256]{2,1,0:T(8,128)}, u32[]{:S(2)}, u32[]{:S(2)}) %all-to-all-start) | async-done | bytes 524320 | tf_op jit(solution)/shard_map/all_to_all | solution.py:27
  44.6 2.1 %collective-permute-start.2 = (f32[128,2048]{1,0:T(8,128)S(1)}, f32[128,2048]{1,0:T(8,128)S(1)}, u32[]{:S(2)}, u32[]{:S(2)}) collective-permute-start(f32[128,2048]{1,0:T(8,128)S(1)} %collective-permute-done.1.green_x_ref), channel_id=1, source_target_pairs={{0,64},{64,0},{1,65},{65,1},{2,66},{66,2},{3,67},{67,3},{4,68},{68... | collective-permute-start | bytes 3145736 | tf_op jit(solution)/shard_map/ppermute | solution.py:19
  46.7 2.3 %collective-permute-done.2.green_xc_ref = f32[128,2048]{1,0:T(8,128)S(1)} collective-permute-done((f32[128,2048]{1,0:T(8,128)S(1)}, f32[128,2048]{1,0:T(8,128)S(1)}, u32[]{:S(2)}, u32[]{:S(2)}) %collective-permute-start.2) | collective-permute-done | bytes 1048608 | tf_op jit(solution)/shard_map/ppermute | solution.py:19
  49.0 1.6 %copy-done.2 = bf16[512,2048]{1,0:T(8,128)(2,1)S(1)} copy-done((bf16[512,2048]{1,0:T(8,128)(2,1)S(1)}, bf16[512,2048]{1,0:T(8,128)(2,1)}, u32[]{:S(2)}) %copy-start.2) | copy-done | bytes 2097176
  50.6 3.0 %shard_map.38 = f32[2,4,64,256]{3,2,1,0:T(8,128)} custom-call(f32[128,2048]{1,0:T(8,128)S(1)} %collective-permute-done.1.green_x_ref, f32[128,2048]{1,0:T(8,128)S(1)} %collective-permute-done.2.green_xc_ref, bf16[512,2048]{1,0:T(8,128)(2,1)S(1)} %copy-done.1, bf16[512,2048]{1,0:T(8,128)(2,1)S(1)} %copy-done.2), custom_call_target="tpu_custom_call" | custom-call | flops 1610612736 | bytes 6291456 | tf_op jit(solution)/shard_map/pallas_call | solution.py:107
  53.7 3.5 %all-to-all-start.1 = ((f32[8,64,256]{2,1,0:T(8,128)}), f32[8,64,256]{2,1,0:T(8,128)S(1)}, u32[]{:S(2)}, u32[]{:S(2)}) async-start(f32[8,64,256]{2,1,0:T(8,128)} %bitcast.2), calls=%async_computation.1 | async-start | bytes 1048576 | tf_op jit(solution)/shard_map/all_to_all | solution.py:27
  57.2 1.1 %reduce_sum.28 = f32[64,256]{1,0:T(8,128)S(1)} reduce(f32[8,64,256]{2,1,0:T(8,128)} %all-to-all-done, f32[]{:T(128)} %constant.19.clone.1), dimensions={0}, to_apply=%region_1.2 | reduce | flops 114688 | bytes 589828 | tf_op jit(solution)/shard_map/reduce_sum | solution.py:150
  58.3 9.8 %all-to-all-done.1 = f32[8,64,256]{2,1,0:T(8,128)S(1)} async-done(((f32[8,64,256]{2,1,0:T(8,128)}), f32[8,64,256]{2,1,0:T(8,128)S(1)}, u32[]{:S(2)}, u32[]{:S(2)}) %all-to-all-start.1) | async-done | bytes 524320 | tf_op jit(solution)/shard_map/all_to_all | solution.py:27
  68.2 0.1 fusion
  68.4 10.1 %all_to_all.20.effective_ref = f32[8,32,128]{2,1,0:T(8,128)S(1)} all-to-all(f32[8,32,128]{2,1,0:T(8,128)S(1)} %bitcast.8), channel_id=1, replica_groups=mesh['xh'=2,'c'=2,'z2'=2,'z1'=2,'z0'=2,'yh'=2,'y0'=2,'xl'=2] {'z2','z1',..., dimensions={0} | all-to-all | bytes 262144 | tf_op jit(solution)/shard_map/all_to_all | solution.py:27
  78.5 1.2 %all-gather.2.cloned.1.call-done.factors_ref = f32[128,4096]{1,0:T(8,128)} async-done(((f32[32,4096]{1,0:T(8,128)}), f32[128,4096]{1,0:T(8,128)}) %all-gather.2.cloned.1.call-update) | async-done | bytes 2097168 | tf_op jit(solution)/shard_map/all_gather | solution.py:144
  79.6 1.6 %copy-done = f32[128,4096]{1,0:T(8,128)S(1)} copy-done((f32[128,4096]{1,0:T(8,128)S(1)}, f32[128,4096]{1,0:T(8,128)}, u32[]{:S(2)}) %copy-start) | copy-done | bytes 2097176
  81.2 1.0 shard_map.39
  82.3 15.1 %all_to_all.21 = f32[16,8,1024]{2,1,0:T(8,128)S(1)} all-to-all(f32[16,8,1024]{2,1,0:T(8,128)S(1)} %shard_map.39), channel_id=1, replica_groups=mesh['xh'=2,'c'=2,'z2'=2,'z1'=2,'z0'=2,'yh'=2,'y0'=2,'xl'=2] {'xh','c','..., dimensions={0} | all-to-all | bytes 1048576 | tf_op jit(solution)/shard_map/all_to_all | solution.py:27
  97.3 0.6 reduce_sum.29
  (19 shorter events, 0.3 us)
Async XLA Ops:
  6.5 7.2 %collective-permute-start = (f32[128,2048]{1,0:T(8,128)}, f32[128,2048]{1,0:T(8,128)S(1)}, u32[]{:S(2)}, u32[]{:S(2)}) collective-permute-start(f32[128,2048]{1,0:T(8,128)} %green_ref.1), channel_id=1, source_target_pairs={{0,64},{64,0},{1,65},{65,1},{2,66},{66,2},{3,67},{67,3},{4,68},{68... | collective-permute-start | bytes 3145736 | tf_op jit(solution)/shard_map/ppermute | solution.py:19
  9.8 26.8 %collective-permute-start.1 = (f32[128,2048]{1,0:T(8,128)}, f32[128,2048]{1,0:T(8,128)S(1)}, u32[]{:S(2)}, u32[]{:S(2)}) collective-permute-start(f32[128,2048]{1,0:T(8,128)} %green_ref.1), channel_id=1, source_target_pairs={{0,128},{128,0},{1,129},{129,1},{2,130},{130,2},{3,131},{131,3},{4... | collective-permute-start | bytes 3145736 | tf_op jit(solution)/shard_map/ppermute | solution.py:19
  10.8 9.7 %collective-permute-start.3 = (f32[8,4096]{1,0:T(8,128)}, f32[8,4096]{1,0:T(8,128)S(1)}, u32[]{:S(2)}, u32[]{:S(2)}) collective-permute-start(f32[8,4096]{1,0:T(8,128)} %param.5), channel_id=1, source_target_pairs={{0,16},{16,0},{1,17},{17,1},{2,18},{18,2},{3,19},{19,3},{4,20},{20... | collective-permute-start | bytes 393224 | tf_op jit(solution)/shard_map/ppermute | solution.py:19
  13.8 1.0 copy-start.3
  14.7 5.7 %copy-start.4 = (f32[8,4096]{1,0:T(8,128)S(1)}, f32[8,4096]{1,0:T(8,128)}, u32[]{:S(2)}) copy-start(f32[8,4096]{1,0:T(8,128)} %param.5) | copy-start | bytes 393220
  20.4 28.6 %copy-start.1 = (bf16[512,2048]{1,0:T(8,128)(2,1)S(1)}, bf16[512,2048]{1,0:T(8,128)(2,1)}, u32[]{:S(2)}) copy-start(bf16[512,2048]{1,0:T(8,128)(2,1)} %get-tuple-element.15.high_ref) | copy-start | bytes 6291460
  20.5 14.2 %collective-permute-start.4 = (f32[16,4096]{1,0:T(8,128)S(1)}, f32[16,4096]{1,0:T(8,128)}, u32[]{:S(2)}, u32[]{:S(2)}) collective-permute-start(f32[16,4096]{1,0:T(8,128)S(1)} %maximum_select_fusion.1), channel_id=1, source_target_pairs={{0,32},{32,0},{1,33},{33,1},{2,34},{34,2},{3,35},{35,3},{4,36},{36... | collective-permute-start | bytes 786440 | tf_op jit(solution)/shard_map/ppermute | solution.py:19
  26.7 17.9 %all-to-all-start = ((f32[8,64,256]{2,1,0:T(8,128)}), f32[8,64,256]{2,1,0:T(8,128)}, u32[]{:S(2)}, u32[]{:S(2)}) async-start(f32[8,64,256]{2,1,0:T(8,128)} %bitcast.7), calls=%async_computation | async-start | bytes 1048576 | tf_op jit(solution)/shard_map/all_to_all | solution.py:27
  30.9 48.7 %all-gather.2.cloned.1.call-start = ((), (), s32[]{:S(2)}) async-start(), calls=%async_computation.4 | async-start | bytes 2621440 | tf_op jit(solution)/shard_map/all_gather | solution.py:144
  44.6 4.4 %collective-permute-start.2 = (f32[128,2048]{1,0:T(8,128)S(1)}, f32[128,2048]{1,0:T(8,128)S(1)}, u32[]{:S(2)}, u32[]{:S(2)}) collective-permute-start(f32[128,2048]{1,0:T(8,128)S(1)} %collective-permute-done.1.green_x_ref), channel_id=1, source_target_pairs={{0,64},{64,0},{1,65},{65,1},{2,66},{66,2},{3,67},{67,3},{4,68},{68... | collective-permute-start | bytes 3145736 | tf_op jit(solution)/shard_map/ppermute | solution.py:19
  49.0 1.6 %copy-start.2 = (bf16[512,2048]{1,0:T(8,128)(2,1)S(1)}, bf16[512,2048]{1,0:T(8,128)(2,1)}, u32[]{:S(2)}) copy-start(bf16[512,2048]{1,0:T(8,128)(2,1)} %get-tuple-element.16.low_ref) | copy-start | bytes 6291460
  53.7 14.4 %all-to-all-start.1 = ((f32[8,64,256]{2,1,0:T(8,128)}), f32[8,64,256]{2,1,0:T(8,128)S(1)}, u32[]{:S(2)}, u32[]{:S(2)}) async-start(f32[8,64,256]{2,1,0:T(8,128)} %bitcast.2), calls=%async_computation.1 | async-start | bytes 1048576 | tf_op jit(solution)/shard_map/all_to_all | solution.py:27
  79.6 1.6 %copy-start = (f32[128,4096]{1,0:T(8,128)S(1)}, f32[128,4096]{1,0:T(8,128)}, u32[]{:S(2)}) copy-start(f32[128,4096]{1,0:T(8,128)} %all-gather.2.cloned.1.call-done.factors_ref) | copy-start | bytes 6291460
Sparse Core Ops, SparseCore 0:
  36.7 42.8 all-gather.1

commit v3 on v2

v3 whole, which is shorter than its diff:
```python
import functools

import jax
import jax.numpy as jnp
from jax import lax
from jax.experimental import pallas as pl
from jax.experimental.pallas import tpu as pltpu
from jax.sharding import Mesh, PartitionSpec as P

SIZES = {"xh": 2, "c": 2, "zh": 4, "z0": 2, "y": 4, "xl": 2}
AXES = tuple(SIZES)
ROW = ("xh", "c")
COL = ("zh", "z0", "y", "xl")
VMEM_BYTES = 56 * 2**20


def move(x, axis):
    return lax.ppermute(x, axis, [(0, 1), (1, 0)])


def from_above(x, axis, steps):
    return lax.ppermute(x, axis, [(i, (i - steps) % 4) for i in range(4)])


def exchange(pieces, axes):
    return lax.all_to_all(pieces, axes, 0, 0, tiled=True)


def halves(x):
    high = x.astype(jnp.bfloat16)
    return high, (x - high.astype(jnp.float32)).astype(jnp.bfloat16)


def dot(x, y, contract):
    return lax.dot_general(x, y, (contract, ((), ())), preferred_element_type=jnp.float32)


def split_walkers(refs, walkers_ref):
    for block, ref in enumerate(refs):
        high, low = halves(ref[...])
        walkers_ref[128 * block : 128 * block + 128] = high
        walkers_ref[256 + 128 * block : 384 + 128 * block] = low


def write_terms(walkers_ref, high, low, out_ref):
    both = dot(walkers_ref[...], high, ((1,), (1,)))
    terms = both[:256] + (both[256:] + dot(walkers_ref[:256], low, ((1,), (1,))))
    for y in range(4):
        for run in range(4):
            out_ref[0, y, 16 * run : 16 * run + 16] = terms[64 * run + 16 * y : 64 * run + 16 * y + 16]


def near_kernel(green_ref, green_c_ref, amplitudes_ref, out_ref, rows_ref, walkers_ref):
    @pl.when(pl.program_id(0) == 0)
    def _():
        split_walkers((green_ref, green_c_ref), walkers_ref)

    for xl in range(2):
        for y in range(4):
            for zh in range(0, 4, 2):
                rows = jnp.concatenate([amplitudes_ref[zh, 0, y, xl], amplitudes_ref[zh + 1, 0, y, xl]])
                high, low = halves(rows)
                start = 128 * xl + 32 * y + 8 * zh
                rows_ref[0, 0, start : start + 16] = high
                rows_ref[0, 1, start : start + 16] = low
    write_terms(walkers_ref, rows_ref[0, 0], rows_ref[0, 1], out_ref)


def far_kernel(green_x_ref, green_xc_ref, rows_ref, out_ref, walkers_ref):
    @pl.when(pl.program_id(0) == 0)
    def _():
        split_walkers((green_x_ref, green_xc_ref), walkers_ref)

    write_terms(walkers_ref, rows_ref[0, 0], rows_ref[0, 1], out_ref)


def bias_kernel(effective_ref, *refs):
    *factor_refs, out_ref = refs
    effective = jnp.sum(effective_ref[...], axis=0)
    effective = pltpu.roll(effective, lax.rem(128 - 32 * lax.axis_index("y"), 128), 1)
    shift = 8 * lax.axis_index("zh")
    lane = lax.broadcasted_iota(jnp.int32, effective.shape, 1)
    effective = jnp.where(
        lax.rem(lane, 32) < 32 - shift,
        pltpu.roll(effective, lax.rem(128 - shift, 128), 1),
        pltpu.roll(effective, 32 - shift, 1),
    )
    high, low = halves(effective)
    own, up, left, right, down = [halves(ref[...]) for ref in factor_refs]
    across = [jnp.concatenate(pair, axis=1) for pair in zip(left, right)]
    parts = [own, up, across, down]
    both = dot(jnp.concatenate([high, low]), jnp.concatenate([part[0] for part in parts]), ((1,), (0,)))
    cross = dot(high, jnp.concatenate([part[1] for part in parts]), ((1,), (0,)))
    bias = (both[:32] + (both[32:] + cross)).reshape(4, 8, 4096)
    for g in range(4):
        out_ref[4 * g : 4 * g + 4] = bias[:, :, 1024 * g : 1024 * g + 1024]


def near_terms(green, green_c, amplitudes):
    pairs = green.shape[1]
    walkers = pl.BlockSpec((128, pairs), lambda g: (0, 0))
    return pl.pallas_call(
        near_kernel,
        out_shape=(
            jax.ShapeDtypeStruct((2, 4, 64, 256), jnp.float32),
            jax.ShapeDtypeStruct((2, 2, 256, pairs), jnp.bfloat16),
        ),
        grid=(2,),
        in_specs=[walkers, walkers, pl.BlockSpec((4, 1, 4, 2, 8, pairs), lambda g: (0, g, 0, 0, 0, 0))],
        out_specs=(
            pl.BlockSpec((1, 4, 64, 256), lambda g: (g, 0, 0, 0)),
            pl.BlockSpec((1, 2, 256, pairs), lambda g: (g, 0, 0, 0)),
        ),
        scratch_shapes=[pltpu.VMEM((512, pairs), jnp.bfloat16)],
        compiler_params=pltpu.CompilerParams(vmem_limit_bytes=VMEM_BYTES),
        cost_estimate=pl.CostEstimate(flops=0, bytes_accessed=0, transcendentals=0),
    )(green, green_c, amplitudes.reshape(4, 2, 4, 2, 8, pairs))


def far_terms(green_x, green_xc, rows):
    pairs = green_x.shape[1]
    walkers = pl.BlockSpec((128, pairs), lambda g: (0, 0))
    return pl.pallas_call(
        far_kernel,
        out_shape=jax.ShapeDtypeStruct((2, 4, 64, 256), jnp.float32),
        grid=(2,),
        in_specs=[walkers, walkers, pl.BlockSpec((1, 2, 256, pairs), lambda g: (g, 0, 0, 0))],
        out_specs=pl.BlockSpec((1, 4, 64, 256), lambda g: (g, 0, 0, 0)),
        scratch_shapes=[pltpu.VMEM((512, pairs), jnp.bfloat16)],
        compiler_params=pltpu.CompilerParams(vmem_limit_bytes=20 * 2**20),
        cost_estimate=pl.CostEstimate(flops=0, bytes_accessed=0, transcendentals=0),
    )(green_x, green_xc, rows)


def bias_terms(effective, factors):
    return pl.pallas_call(
        bias_kernel,
        out_shape=jax.ShapeDtypeStruct((16, 8, 1024), jnp.float32),
        grid=(1,),
        in_specs=[pl.BlockSpec((8, 32, 128), lambda g: (0, 0, 0))] + [pl.BlockSpec(factor.shape, lambda g: (0, 0)) for factor in factors],
        out_specs=pl.BlockSpec((16, 8, 1024), lambda g: (0, 0, 0)),
        compiler_params=pltpu.CompilerParams(vmem_limit_bytes=VMEM_BYTES),
        cost_estimate=pl.CostEstimate(flops=6 * 32 * 128 * 4096, bytes_accessed=3 * 2**20, transcendentals=0),
    )(effective, *factors)


def per_device(green, amplitudes, cholesky):
    green_x = move(green, "xh")
    green_c = move(green, "c")
    others = [from_above(cholesky, "zh", k) for k in (1, 2, 3)]

    near, rows = near_terms(green, green_c, amplitudes)
    near = exchange(near.reshape(8, 64, 256), ("z0", "y"))
    owned = jnp.concatenate([cholesky] + others)
    up, down = from_above(owned, "y", 1), from_above(owned, "y", 3)
    near, green_x, owned = lax.optimization_barrier((near, green_x, owned))
    far = far_terms(green_x, move(green_x, "c"), rows)
    far, up, down = lax.optimization_barrier((far, up, down))
    left, right = from_above(up[:, :2048], "y", 1), from_above(down[:, 2048:], "y", 3)
    far = exchange(far.reshape(8, 64, 256), ("z0", "y"))
    factors = [owned, up, left, right, down]

    near = jnp.sum(near, axis=0).reshape(2, 32, 2, 128)
    far = jnp.sum(far, axis=0).reshape(2, 32, 2, 128)
    blocks = jnp.concatenate([near, far])
    blocks = jnp.where(lax.axis_index("xh") == 1, jnp.concatenate([far, near]), blocks)
    swapped = jnp.stack([blocks[1], blocks[0], blocks[3], blocks[2]])
    blocks = jnp.where(lax.axis_index("c") == 1, swapped, blocks)
    effective = exchange(blocks.transpose(0, 2, 1, 3).reshape(8, 32, 128), ("zh", "xl"))

    bias = exchange(bias_terms(effective, factors), ("xh", "c", "z0", "xl"))
    return jnp.sum(bias, axis=0)


def solution(mesh):
    parts = Mesh(mesh.devices.reshape(tuple(SIZES.values())), AXES)
    return jax.shard_map(
        per_device,
        mesh=parts,
        in_specs=(P(ROW, COL), P(ROW, COL), P(AXES, None)),
        out_specs=P(COL, ROW),
        check_vma=False,
    )
```

time: 105 us -> 98.2 us (0.935)
  between operations: 13.5 us -> 0.19 us
  starting transfers between devices: 23.3 us -> 32.8 us
  blocking collectives: 25.2 us -> 18.3 us
  waiting for transfers between devices: 25 us -> 28.2 us
  other arithmetic: 3.81 us -> 0.88 us
  Pallas kernels: 9.75 us -> 11.7 us
  local copies, waits for them, and re-layouts: 4.24 us -> 5.58 us
    ppermute x0 -> x7, starting transfers between devices: none -> 13.5 us  [from_above(): return lax.ppermute(x, axis, [(i, (i - steps) % 4) for i in range(4)])]
    ppermute x0 -> x7, waiting for transfers between devices: none -> 10.6 us  [from_above(): return lax.ppermute(x, axis, [(i, (i - steps) % 4) for i in range(4)])]
    ppermute x5 -> x3, starting transfers between devices: 15.6 us -> 7.47 us  [move(): return lax.ppermute(x, axis, [(0, 1), (1, 0)])]
    all_to_all x2 -> x1, blocking collectives: 25.2 us -> 18.3 us  [exchange(): return lax.all_to_all(pieces, axes, 0, 0, tiled=True)]
    all_to_all x2 -> x3, waiting for transfers between devices: 17.8 us -> 13 us  [exchange(): return lax.all_to_all(pieces, axes, 0, 0, tiled=True)]
    all_to_all x2 -> x3, starting transfers between devices: 7.68 us -> 11.8 us  [exchange(): return lax.all_to_all(pieces, axes, 0, 0, tiled=True)]
    pallas_call x1, Pallas kernels: 1.04 us -> 3.01 us  [bias_terms(): pl.pallas_call(bias_kernel, out_shape=jax.ShapeDtypeStruct((16, 8, 1024),...]
    select_n x2 -> x0, other arithmetic: 1.89 us -> none  [in_order(): jnp.where(lax.axis_index(axis) == 1, jnp.concatenate([other, x]), jnp.con...]
  transfers between devices with their start and end apart: 8 -> 13, of which waited for: 5 -> 9; matrix products, arithmetic and copies ran while one was open for 3% -> 2% of each run, Pallas kernels for 8% -> 9%
where the time goes in v3:
time: 98.2 us; the launch traced here: 97.7 us
  starting transfers between devices  32.8 us (33%)
  waiting for transfers between devices  28.2 us (29%)
  blocking collectives  18.3 us (19%)
  Pallas kernels  11.7 us (12%)
  local copies, waits for them, and re-layouts  5.58 us (6%)
    all_to_all x1, blocking collectives, exchange(): return lax.all_to_all(pieces, axes, 0, 0, tiled=True)  18.3 us
    ppermute x7, starting transfers between devices, from_above(): return lax.ppermute(x, axis, [(i, (i - steps) % 4) for i in range(4)])  13.5 us
    all_to_all x3, waiting for transfers between devices, exchange(): return lax.all_to_all(pieces, axes, 0, 0, tiled=True)  13 us
    all_to_all x3, starting transfers between devices, exchange(): return lax.all_to_all(pieces, axes, 0, 0, tiled=True)  11.8 us
    ppermute x7, waiting for transfers between devices, from_above(): return lax.ppermute(x, axis, [(i, (i - steps) % 4) for i in range(4)])  10.6 us
    ppermute x3, starting transfers between devices, move(): return lax.ppermute(x, axis, [(0, 1), (1, 0)])  7.47 us
    pallas_call x1, Pallas kernels, near_terms(): pl.pallas_call(near_kernel, out_shape=(jax.ShapeDtypeStruct((2, 4, 64, 25...  5.72 us
    unnamed x19, local copies, waits for them, and re-layouts  4.79 us
  transfers between devices with their start and end apart: 13, of which 9 were waited for; matrix products, arithmetic and copies ran while one was open for 2% of the time, Pallas kernels for 9%

profile of v3, /device:TPU:1, one launch (start us, length us, event | category | flops | bytes accessed | tf_op | source)
XLA Modules:
  0.0 97.7 jit_solution(2874314433554595840)
XLA Ops:
  0.0 3.2 %collective-permute-start = (f32[128,2048]{1,0:T(8,128)}, f32[128,2048]{1,0:T(8,128)S(1)}, u32[]{:S(2)}, u32[]{:S(2)}) collective-permute-start(f32[128,2048]{1,0:T(8,128)} %green_ref.1), channel_id=1, source_target_pairs={{0,64},{64,0},{1,65},{65,1},{2,66},{66,2},{3,67},{67,3},{4,68},{68... | collective-permute-start | bytes 3145736 | tf_op jit(solution)/shard_map/ppermute | solution.py:18
  3.2 1.0 %collective-permute-start.1 = (f32[128,2048]{1,0:T(8,128)}, f32[128,2048]{1,0:T(8,128)S(1)}, u32[]{:S(2)}, u32[]{:S(2)}) collective-permute-start(f32[128,2048]{1,0:T(8,128)} %green_ref.1), channel_id=1, source_target_pairs={{0,128},{128,0},{1,129},{129,1},{2,130},{130,2},{3,131},{131,3},{4... | collective-permute-start | bytes 3145736 | tf_op jit(solution)/shard_map/ppermute | solution.py:18
  4.2 6.0 %collective-permute-start.2 = (f32[8,4096]{1,0:T(8,128)}, f32[8,4096]{1,0:T(8,128)S(1)}, u32[]{:S(2)}, u32[]{:S(2)}) collective-permute-start(f32[8,4096]{1,0:T(8,128)} %param.5), channel_id=1, source_target_pairs={{0,48},{16,0},{32,16},{48,32},{1,49},{17,1},{33,17},{49,33},{2,50}... | collective-permute-start | bytes 393224 | tf_op jit(solution)/shard_map/ppermute | solution.py:22
  10.3 0.9 collective-permute-start.3
  11.2 2.4 %collective-permute-start.4 = (f32[8,4096]{1,0:T(8,128)}, f32[8,4096]{1,0:T(8,128)S(1)}, u32[]{:S(2)}, u32[]{:S(2)}) collective-permute-start(f32[8,4096]{1,0:T(8,128)} %param.5), channel_id=1, source_target_pairs={{0,16},{16,32},{32,48},{48,0},{1,17},{17,33},{33,49},{49,1},{2,18}... | collective-permute-start | bytes 393224 | tf_op jit(solution)/shard_map/ppermute | solution.py:22
  13.5 0.9 constant_dynamic-update-slice_fusion.3
  14.5 1.0 copy-done.3
  15.5 5.7 %shard_map.37 = (f32[2,4,64,256]{3,2,1,0:T(8,128)}, bf16[2,2,256,2048]{3,2,1,0:T(8,128)(2,1)}) custom-call(f32[128,2048]{1,0:T(8,128)} %green_ref.1, f32[128,2048]{1,0:T(8,128)} %copy-done.3, f32[4,2,4,2,8,2048]{5,4,3,2,1,0:T(8,128)} %bitcast.6), custom_call_target="tpu_custom_call" | custom-call | tf_op jit(solution)/shard_map/pallas_call | solution.py:102
  21.2 4.6 %all-to-all-start = ((f32[8,64,256]{2,1,0:T(8,128)}), f32[8,64,256]{2,1,0:T(8,128)S(1)}, u32[]{:S(2)}, u32[]{:S(2)}) async-start(f32[8,64,256]{2,1,0:T(8,128)} %bitcast.7), calls=%async_computation | async-start | bytes 1048576 | tf_op jit(solution)/shard_map/all_to_all | solution.py:26
  25.9 3.8 %collective-permute-done.1.green_x_ref = f32[128,2048]{1,0:T(8,128)S(1)} collective-permute-done((f32[128,2048]{1,0:T(8,128)}, f32[128,2048]{1,0:T(8,128)S(1)}, u32[]{:S(2)}, u32[]{:S(2)}) %collective-permute-start.1) | collective-permute-done | bytes 1048608 | tf_op jit(solution)/shard_map/ppermute | solution.py:18
  29.7 3.5 %all-to-all-done = f32[8,64,256]{2,1,0:T(8,128)S(1)} async-done(((f32[8,64,256]{2,1,0:T(8,128)}), f32[8,64,256]{2,1,0:T(8,128)S(1)}, u32[]{:S(2)}, u32[]{:S(2)}) %all-to-all-start) | async-done | bytes 524320 | tf_op jit(solution)/shard_map/all_to_all | solution.py:26
  33.2 3.2 %collective-permute-start.5 = (f32[128,2048]{1,0:T(8,128)S(1)}, f32[128,2048]{1,0:T(8,128)S(1)}, u32[]{:S(2)}, u32[]{:S(2)}) collective-permute-start(f32[128,2048]{1,0:T(8,128)S(1)} %collective-permute-done.1.green_x_ref), channel_id=1, source_target_pairs={{0,64},{64,0},{1,65},{65,1},{2,66},{66,2},{3,67},{67,3},{4,68},{68... | collective-permute-start | bytes 3145736 | tf_op jit(solution)/shard_map/ppermute | solution.py:18
  38.7 2.2 %copy-done = bf16[2,2,256,2048]{3,2,1,0:T(8,128)(2,1)S(1)} copy-done((bf16[2,2,256,2048]{3,2,1,0:T(8,128)(2,1)S(1)}, bf16[2,2,256,2048]{3,2,1,0:T(8,128)(2,1)}, u32[]{:S(2)}) %copy-start) | copy-done | bytes 4194328
  40.9 3.0 %shard_map.38 = f32[2,4,64,256]{3,2,1,0:T(8,128)} custom-call(f32[128,2048]{1,0:T(8,128)S(1)} %collective-permute-done.1.green_x_ref, f32[128,2048]{1,0:T(8,128)S(1)} %collective-permute-done.5.green_xc_ref, bf16[2,2,256,2048]{3,2,1,0:T(8,128)(2,1)S(1)} %copy-done), custom_call_target="tpu_custom_call" | custom-call | tf_op jit(solution)/shard_map/pallas_call | solution.py:123
  43.9 6.1 %collective-permute-done.6.refs_1_ = f32[32,4096]{1,0:T(8,128)S(1)} collective-permute-done((f32[32,4096]{1,0:T(8,128)S(1)}, f32[32,4096]{1,0:T(8,128)S(1)}, u32[]{:S(2)}, u32[]{:S(2)}) %collective-permute-start.6) | collective-permute-done | bytes 524320 | tf_op jit(solution)/shard_map/ppermute | solution.py:22
  50.0 1.6 %collective-permute-done.7.refs_4_ = f32[32,4096]{1,0:T(8,128)S(1)} collective-permute-done((f32[32,4096]{1,0:T(8,128)S(1)}, f32[32,4096]{1,0:T(8,128)S(1)}, u32[]{:S(2)}, u32[]{:S(2)}) %collective-permute-start.7) | collective-permute-done | bytes 524320 | tf_op jit(solution)/shard_map/ppermute | solution.py:22
  51.6 3.5 %all-to-all-start.1 = ((f32[8,64,256]{2,1,0:T(8,128)}), f32[8,64,256]{2,1,0:T(8,128)S(1)}, u32[]{:S(2)}, u32[]{:S(2)}) async-start(f32[8,64,256]{2,1,0:T(8,128)} %bitcast.2), calls=%async_computation.1 | async-start | bytes 1048576 | tf_op jit(solution)/shard_map/all_to_all | solution.py:26
  55.3 2.6 %collective-permute-start.8 = (f32[32,2048]{1,0:T(8,128)S(1)}, f32[32,2048]{1,0:T(8,128)S(1)}, u32[]{:S(2)}, u32[]{:S(2)}) collective-permute-start(f32[32,2048]{1,0:T(8,128)S(1)} %slice.22), channel_id=1, source_target_pairs={{0,6},{2,0},{4,2},{6,4},{1,7},{3,1},{5,3},{7,5},{8,14},{10,8},{12,... | collective-permute-start | bytes 786440 | tf_op jit(solution)/shard_map/ppermute | solution.py:22
  58.0 4.7 %all-to-all-done.1 = f32[8,64,256]{2,1,0:T(8,128)S(1)} async-done(((f32[8,64,256]{2,1,0:T(8,128)}), f32[8,64,256]{2,1,0:T(8,128)S(1)}, u32[]{:S(2)}, u32[]{:S(2)}) %all-to-all-start.1) | async-done | bytes 524320 | tf_op jit(solution)/shard_map/all_to_all | solution.py:26
  63.7 3.7 %all-to-all-start.2 = ((f32[8,32,128]{2,1,0:T(8,128)}), f32[8,32,128]{2,1,0:T(8,128)S(1)}, u32[]{:S(2)}, u32[]{:S(2)}) async-start(f32[8,32,128]{2,1,0:T(8,128)} %bitcast.4), calls=%async_computation.2 | async-start | bytes 262144 | tf_op jit(solution)/shard_map/all_to_all | solution.py:26
  68.1 2.2 %collective-permute-done.9.refs_3_ = f32[32,2048]{1,0:T(8,128)S(1)} collective-permute-done((f32[32,2048]{1,0:T(8,128)S(1)}, f32[32,2048]{1,0:T(8,128)S(1)}, u32[]{:S(2)}, u32[]{:S(2)}) %collective-permute-start.9) | collective-permute-done | bytes 262176 | tf_op jit(solution)/shard_map/ppermute | solution.py:22
  70.3 4.7 %all-to-all-done.2.effective_ref = f32[8,32,128]{2,1,0:T(8,128)S(1)} async-done(((f32[8,32,128]{2,1,0:T(8,128)}), f32[8,32,128]{2,1,0:T(8,128)S(1)}, u32[]{:S(2)}, u32[]{:S(2)}) %all-to-all-start.2) | async-done | bytes 131104 | tf_op jit(solution)/shard_map/all_to_all | solution.py:26
  75.7 3.0 %shard_map.39 = f32[16,8,1024]{2,1,0:T(8,128)} custom-call(f32[8,32,128]{2,1,0:T(8,128)} %copy-done.5, f32[32,4096]{1,0:T(8,128)} %copy-done.4, f32[32,4096]{1,0:T(8,128)} %copy-done.1, f32[32,2048]{1,0:T(8,128)} %copy-done.6, f32[32,2048]{1,0:T(8,128)} %copy-done.7, f32[32,4096]{1,0:T(8,128)} %copy-done.2), custom_call_target="tpu_custom_call" | custom-call | flops 100663296 | bytes 3145728 | tf_op jit(solution)/shard_map/pallas_call | solution.py:136
  78.7 18.3 %all_to_all.20 = f32[16,8,1024]{2,1,0:T(8,128)S(1)} all-to-all(f32[16,8,1024]{2,1,0:T(8,128)} %shard_map.39), channel_id=1, replica_groups=mesh['xh'=2,'c'=2,'zh'=4,'z0'=2,'y'=4,'xl'=2] {'xh','c','z0','xl'}, dimensions={0} | all-to-all | bytes 1048576 | tf_op jit(solution)/shard_map/all_to_all | solution.py:26
  (37 shorter events, 5.4 us)
Async XLA Ops:
  0.0 14.5 %collective-permute-start = (f32[128,2048]{1,0:T(8,128)}, f32[128,2048]{1,0:T(8,128)S(1)}, u32[]{:S(2)}, u32[]{:S(2)}) collective-permute-start(f32[128,2048]{1,0:T(8,128)} %green_ref.1), channel_id=1, source_target_pairs={{0,64},{64,0},{1,65},{65,1},{2,66},{66,2},{3,67},{67,3},{4,68},{68... | collective-permute-start | bytes 3145736 | tf_op jit(solution)/shard_map/ppermute | solution.py:18
  3.2 26.5 %collective-permute-start.1 = (f32[128,2048]{1,0:T(8,128)}, f32[128,2048]{1,0:T(8,128)S(1)}, u32[]{:S(2)}, u32[]{:S(2)}) collective-permute-start(f32[128,2048]{1,0:T(8,128)} %green_ref.1), channel_id=1, source_target_pairs={{0,128},{128,0},{1,129},{129,1},{2,130},{130,2},{3,131},{131,3},{4... | collective-permute-start | bytes 3145736 | tf_op jit(solution)/shard_map/ppermute | solution.py:18
  4.2 21.6 %collective-permute-start.2 = (f32[8,4096]{1,0:T(8,128)}, f32[8,4096]{1,0:T(8,128)S(1)}, u32[]{:S(2)}, u32[]{:S(2)}) collective-permute-start(f32[8,4096]{1,0:T(8,128)} %param.5), channel_id=1, source_target_pairs={{0,48},{16,0},{32,16},{48,32},{1,49},{17,1},{33,17},{49,33},{2,50}... | collective-permute-start | bytes 393224 | tf_op jit(solution)/shard_map/ppermute | solution.py:22
  10.3 15.6 %collective-permute-start.3 = (f32[8,4096]{1,0:T(8,128)}, f32[8,4096]{1,0:T(8,128)S(1)}, u32[]{:S(2)}, u32[]{:S(2)}) collective-permute-start(f32[8,4096]{1,0:T(8,128)} %param.5), channel_id=1, source_target_pairs={{0,32},{16,48},{32,0},{48,16},{1,33},{17,49},{33,1},{49,17},{2,34}... | collective-permute-start | bytes 393224 | tf_op jit(solution)/shard_map/ppermute | solution.py:22
  11.2 14.7 %collective-permute-start.4 = (f32[8,4096]{1,0:T(8,128)}, f32[8,4096]{1,0:T(8,128)S(1)}, u32[]{:S(2)}, u32[]{:S(2)}) collective-permute-start(f32[8,4096]{1,0:T(8,128)} %param.5), channel_id=1, source_target_pairs={{0,16},{16,32},{32,48},{48,0},{1,17},{17,33},{33,49},{49,1},{2,18}... | collective-permute-start | bytes 393224 | tf_op jit(solution)/shard_map/ppermute | solution.py:22
  14.5 1.0 %copy-start.3 = (f32[128,2048]{1,0:T(8,128)}, f32[128,2048]{1,0:T(8,128)S(1)}, u32[]{:S(2)}) copy-start(f32[128,2048]{1,0:T(8,128)S(1)} %collective-permute-done.green_c_ref) | copy-start | bytes 3145732
  21.2 12.0 %all-to-all-start = ((f32[8,64,256]{2,1,0:T(8,128)}), f32[8,64,256]{2,1,0:T(8,128)S(1)}, u32[]{:S(2)}, u32[]{:S(2)}) async-start(f32[8,64,256]{2,1,0:T(8,128)} %bitcast.7), calls=%async_computation | async-start | bytes 1048576 | tf_op jit(solution)/shard_map/all_to_all | solution.py:26
  25.9 29.3 %copy-start.4 = (f32[32,4096]{1,0:T(8,128)}, f32[32,4096]{1,0:T(8,128)S(1)}, u32[]{:S(2)}) copy-start(f32[32,4096]{1,0:T(8,128)S(1)} %constant_dynamic-update-slice_fusion.refs_0_) | copy-start | bytes 1572868
  33.2 5.5 %collective-permute-start.5 = (f32[128,2048]{1,0:T(8,128)S(1)}, f32[128,2048]{1,0:T(8,128)S(1)}, u32[]{:S(2)}, u32[]{:S(2)}) collective-permute-start(f32[128,2048]{1,0:T(8,128)S(1)} %collective-permute-done.1.green_x_ref), channel_id=1, source_target_pairs={{0,64},{64,0},{1,65},{65,1},{2,66},{66,2},{3,67},{67,3},{4,68},{68... | collective-permute-start | bytes 3145736 | tf_op jit(solution)/shard_map/ppermute | solution.py:18
  36.5 13.6 %collective-permute-start.6 = (f32[32,4096]{1,0:T(8,128)S(1)}, f32[32,4096]{1,0:T(8,128)S(1)}, u32[]{:S(2)}, u32[]{:S(2)}) collective-permute-start(f32[32,4096]{1,0:T(8,128)S(1)} %constant_dynamic-update-slice_fusion.refs_0_), channel_id=1, source_target_pairs={{0,6},{2,0},{4,2},{6,4},{1,7},{3,1},{5,3},{7,5},{8,14},{10,8},{12,... | collective-permute-start | bytes 1572872 | tf_op jit(solution)/shard_map/ppermute | solution.py:22
  37.2 14.4 %collective-permute-start.7 = (f32[32,4096]{1,0:T(8,128)S(1)}, f32[32,4096]{1,0:T(8,128)S(1)}, u32[]{:S(2)}, u32[]{:S(2)}) collective-permute-start(f32[32,4096]{1,0:T(8,128)S(1)} %constant_dynamic-update-slice_fusion.refs_0_), channel_id=1, source_target_pairs={{0,2},{2,4},{4,6},{6,0},{1,3},{3,5},{5,7},{7,1},{8,10},{10,12},{12... | collective-permute-start | bytes 1572872 | tf_op jit(solution)/shard_map/ppermute | solution.py:22
  38.7 2.2 %copy-start = (bf16[2,2,256,2048]{3,2,1,0:T(8,128)(2,1)S(1)}, bf16[2,2,256,2048]{3,2,1,0:T(8,128)(2,1)}, u32[]{:S(2)}) copy-start(bf16[2,2,256,2048]{3,2,1,0:T(8,128)(2,1)} %get-tuple-element.15.rows_ref) | copy-start | bytes 12582916
  50.0 25.0 %copy-start.1 = (f32[32,4096]{1,0:T(8,128)}, f32[32,4096]{1,0:T(8,128)S(1)}, u32[]{:S(2)}) copy-start(f32[32,4096]{1,0:T(8,128)S(1)} %collective-permute-done.6.refs_1_) | copy-start | bytes 1572868
  51.6 23.4 %copy-start.2 = (f32[32,4096]{1,0:T(8,128)}, f32[32,4096]{1,0:T(8,128)S(1)}, u32[]{:S(2)}) copy-start(f32[32,4096]{1,0:T(8,128)S(1)} %collective-permute-done.7.refs_4_) | copy-start | bytes 1572868
  51.6 11.1 %all-to-all-start.1 = ((f32[8,64,256]{2,1,0:T(8,128)}), f32[8,64,256]{2,1,0:T(8,128)S(1)}, u32[]{:S(2)}, u32[]{:S(2)}) async-start(f32[8,64,256]{2,1,0:T(8,128)} %bitcast.2), calls=%async_computation.1 | async-start | bytes 1048576 | tf_op jit(solution)/shard_map/all_to_all | solution.py:26
  55.3 12.8 %collective-permute-start.8 = (f32[32,2048]{1,0:T(8,128)S(1)}, f32[32,2048]{1,0:T(8,128)S(1)}, u32[]{:S(2)}, u32[]{:S(2)}) collective-permute-start(f32[32,2048]{1,0:T(8,128)S(1)} %slice.22), channel_id=1, source_target_pairs={{0,6},{2,0},{4,2},{6,4},{1,7},{3,1},{5,3},{7,5},{8,14},{10,8},{12,... | collective-permute-start | bytes 786440 | tf_op jit(solution)/shard_map/ppermute | solution.py:22
  57.9 12.4 %collective-permute-start.9 = (f32[32,2048]{1,0:T(8,128)S(1)}, f32[32,2048]{1,0:T(8,128)S(1)}, u32[]{:S(2)}, u32[]{:S(2)}) collective-permute-start(f32[32,2048]{1,0:T(8,128)S(1)} %slice.23), channel_id=1, source_target_pairs={{0,2},{2,4},{4,6},{6,0},{1,3},{3,5},{5,7},{7,1},{8,10},{10,12},{12... | collective-permute-start | bytes 786440 | tf_op jit(solution)/shard_map/ppermute | solution.py:22
  63.7 11.3 %all-to-all-start.2 = ((f32[8,32,128]{2,1,0:T(8,128)}), f32[8,32,128]{2,1,0:T(8,128)S(1)}, u32[]{:S(2)}, u32[]{:S(2)}) async-start(f32[8,32,128]{2,1,0:T(8,128)} %bitcast.4), calls=%async_computation.2 | async-start | bytes 262144 | tf_op jit(solution)/shard_map/all_to_all | solution.py:26
  68.1 7.0 %copy-start.6 = (f32[32,2048]{1,0:T(8,128)}, f32[32,2048]{1,0:T(8,128)S(1)}, u32[]{:S(2)}) copy-start(f32[32,2048]{1,0:T(8,128)S(1)} %collective-permute-done.8.refs_2_) | copy-start | bytes 786436
  70.3 4.8 %copy-start.7 = (f32[32,2048]{1,0:T(8,128)}, f32[32,2048]{1,0:T(8,128)S(1)}, u32[]{:S(2)}) copy-start(f32[32,2048]{1,0:T(8,128)S(1)} %collective-permute-done.9.refs_3_) | copy-start | bytes 786436
  75.1 0.7 copy-start.5

commit v4 on v3

--- a/solution.py
+++ b/solution.py
@@ -75,7 +75,7 @@
 
 
 def bias_kernel(effective_ref, *refs):
-    *factor_refs, out_ref = refs
+    *factor_refs, mine_ref, theirs_ref = refs
     effective = jnp.sum(effective_ref[...], axis=0)
     effective = pltpu.roll(effective, lax.rem(128 - 32 * lax.axis_index("y"), 128), 1)
     shift = 8 * lax.axis_index("zh")
@@ -92,8 +92,14 @@
     both = dot(jnp.concatenate([high, low]), jnp.concatenate([part[0] for part in parts]), ((1,), (0,)))
     cross = dot(high, jnp.concatenate([part[1] for part in parts]), ((1,), (0,)))
     bias = (both[:32] + (both[32:] + cross)).reshape(4, 8, 4096)
-    for g in range(4):
-        out_ref[4 * g : 4 * g + 4] = bias[:, :, 1024 * g : 1024 * g + 1024]
+    for core in range(2):
+
+        @pl.when(lax.axis_index("c") == core)
+        def _():
+            for xh in range(2):
+                for ref, to in ((mine_ref, core), (theirs_ref, 1 - core)):
+                    start = 1024 * (2 * xh + to)
+                    ref[4 * xh : 4 * xh + 4] = bias[:, :, start : start + 1024]
 
 
 def near_terms(green, green_c, amplitudes):
@@ -133,15 +139,20 @@
 
 
 def bias_terms(effective, factors):
+    whole = pl.BlockSpec(memory_space=pltpu.VMEM)
+    piece = jax.ShapeDtypeStruct((8, 8, 1024), jnp.float32)
     return pl.pallas_call(
         bias_kernel,
-        out_shape=jax.ShapeDtypeStruct((16, 8, 1024), jnp.float32),
-        grid=(1,),
-        in_specs=[pl.BlockSpec((8, 32, 128), lambda g: (0, 0, 0))] + [pl.BlockSpec(factor.shape, lambda g: (0, 0)) for factor in factors],
-        out_specs=pl.BlockSpec((16, 8, 1024), lambda g: (0, 0, 0)),
-        compiler_params=pltpu.CompilerParams(vmem_limit_bytes=VMEM_BYTES),
+        out_shape=(piece, piece),
+        in_specs=[whole] * (1 + len(factors)),
+        out_specs=(whole, whole),
+        compiler_params=pltpu.CompilerParams(vmem_limit_bytes=16 * 2**20),
         cost_estimate=pl.CostEstimate(flops=6 * 32 * 128 * 4096, bytes_accessed=3 * 2**20, transcendentals=0),
     )(effective, *factors)
+
+
+def by_row_part(terms):
+    return jnp.stack([terms[:, :128].reshape(2, 32, 128), terms[:, 128:].reshape(2, 32, 128)], axis=1)
 
 
 def per_device(green, amplitudes, cholesky):
@@ -160,15 +171,15 @@
     far = exchange(far.reshape(8, 64, 256), ("z0", "y"))
     factors = [owned, up, left, right, down]
 
-    near = jnp.sum(near, axis=0).reshape(2, 32, 2, 128)
-    far = jnp.sum(far, axis=0).reshape(2, 32, 2, 128)
+    near, far = by_row_part(jnp.sum(near, axis=0)), by_row_part(jnp.sum(far, axis=0))
     blocks = jnp.concatenate([near, far])
     blocks = jnp.where(lax.axis_index("xh") == 1, jnp.concatenate([far, near]), blocks)
     swapped = jnp.stack([blocks[1], blocks[0], blocks[3], blocks[2]])
     blocks = jnp.where(lax.axis_index("c") == 1, swapped, blocks)
-    effective = exchange(blocks.transpose(0, 2, 1, 3).reshape(8, 32, 128), ("zh", "xl"))
+    effective = exchange(blocks.reshape(8, 32, 128), ("zh", "xl"))
 
-    bias = exchange(bias_terms(effective, factors), ("xh", "c", "z0", "xl"))
+    mine, theirs = bias_terms(effective, factors)
+    bias = exchange(mine + move(theirs, "c"), ("xh", "z0", "xl"))
     return jnp.sum(bias, axis=0)
 
 

time: 98.2 us -> 95 us (0.967)
  blocking collectives: 18.3 us -> 10.5 us
  starting transfers between devices: 32.8 us -> 38.2 us
  Pallas kernels: 11.7 us -> 9.41 us
  other arithmetic: 0.88 us -> 2.48 us
  local copies, waits for them, and re-layouts: 5.58 us -> 4.19 us
  waiting for transfers between devices: 28.2 us -> 29.5 us
    all_to_all x1, blocking collectives: 18.3 us -> 10.5 us  [exchange(): return lax.all_to_all(pieces, axes, 0, 0, tiled=True)]
    ppermute x3 -> x4, starting transfers between devices: 7.47 us -> 12.3 us  [move(): return lax.ppermute(x, axis, [(0, 1), (1, 0)])]
    pallas_call x1, Pallas kernels: 3.01 us -> 0.67 us  [bias_terms(): pl.pallas_call(bias_kernel, out_shape=(piece, piece), in_specs=[whole] *...]
    ppermute x3 -> x4, waiting for transfers between devices: 4.65 us -> 5.84 us  [move(): return lax.ppermute(x, axis, [(0, 1), (1, 0)])]
    all_to_all x3, waiting for transfers between devices: 13 us -> 14.1 us  [exchange(): return lax.all_to_all(pieces, axes, 0, 0, tiled=True)]
    reduce_sum x2, other arithmetic: 0.07 us -> 1.12 us  [the longest x1 1.08 us: per_device(): jnp.sum(far, axis=0)]
    ppermute x7, waiting for transfers between devices: 10.6 us -> 9.55 us  [from_above(): return lax.ppermute(x, axis, [(i, (i - steps) % 4) for i in range(4)])]
    unnamed x19 -> x7, local copies, waits for them, and re-layouts: 4.79 us -> 4.12 us
  transfers between devices with their start and end apart: 13 -> 14, of which waited for: 9 -> 9; matrix products, arithmetic and copies ran while one was open for 2% -> 3% of each run, Pallas kernels for 9% -> 9%
where the time goes in v4:
time: 95 us; the launch traced here: 94.5 us
  starting transfers between devices  38.2 us (40%)
  waiting for transfers between devices  29.5 us (31%)
  blocking collectives  10.5 us (11%)
  Pallas kernels  9.41 us (10%)
  local copies, waits for them, and re-layouts  4.19 us (4%)
  other arithmetic  2.48 us (3%)
    all_to_all x3, waiting for transfers between devices, exchange(): return lax.all_to_all(pieces, axes, 0, 0, tiled=True)  14.1 us
    ppermute x7, starting transfers between devices, from_above(): return lax.ppermute(x, axis, [(i, (i - steps) % 4) for i in range(4)])  13.4 us
    all_to_all x3, starting transfers between devices, exchange(): return lax.all_to_all(pieces, axes, 0, 0, tiled=True)  12.5 us
    ppermute x4, starting transfers between devices, move(): return lax.ppermute(x, axis, [(0, 1), (1, 0)])  12.3 us
    all_to_all x1, blocking collectives, exchange(): return lax.all_to_all(pieces, axes, 0, 0, tiled=True)  10.5 us
    ppermute x7, waiting for transfers between devices, from_above(): return lax.ppermute(x, axis, [(i, (i - steps) % 4) for i in range(4)])  9.55 us
    ppermute x4, waiting for transfers between devices, move(): return lax.ppermute(x, axis, [(0, 1), (1, 0)])  5.84 us
    pallas_call x1, Pallas kernels, near_terms(): pl.pallas_call(near_kernel, out_shape=(jax.ShapeDtypeStruct((2, 4, 64, 25...  5.71 us
  transfers between devices with their start and end apart: 14, of which 9 were waited for; matrix products, arithmetic and copies ran while one was open for 3% of the time, Pallas kernels for 9%

profile of v4, /device:TPU:1, one launch (start us, length us, event | category | flops | bytes accessed | tf_op | source)
XLA Modules:
  0.0 94.5 jit_solution(14273870409403653766)
XLA Ops:
  0.0 3.2 %collective-permute-start = (f32[128,2048]{1,0:T(8,128)}, f32[128,2048]{1,0:T(8,128)S(1)}, u32[]{:S(2)}, u32[]{:S(2)}) collective-permute-start(f32[128,2048]{1,0:T(8,128)} %green_ref.1), channel_id=1, source_target_pairs={{0,64},{64,0},{1,65},{65,1},{2,66},{66,2},{3,67},{67,3},{4,68},{68... | collective-permute-start | bytes 3145736 | tf_op jit(solution)/shard_map/ppermute | solution.py:18
  3.2 1.0 %collective-permute-start.1 = (f32[128,2048]{1,0:T(8,128)}, f32[128,2048]{1,0:T(8,128)S(1)}, u32[]{:S(2)}, u32[]{:S(2)}) collective-permute-start(f32[128,2048]{1,0:T(8,128)} %green_ref.1), channel_id=1, source_target_pairs={{0,128},{128,0},{1,129},{129,1},{2,130},{130,2},{3,131},{131,3},{4... | collective-permute-start | bytes 3145736 | tf_op jit(solution)/shard_map/ppermute | solution.py:18
  4.2 6.0 %collective-permute-start.2 = (f32[8,4096]{1,0:T(8,128)}, f32[8,4096]{1,0:T(8,128)S(1)}, u32[]{:S(2)}, u32[]{:S(2)}) collective-permute-start(f32[8,4096]{1,0:T(8,128)} %param.5), channel_id=1, source_target_pairs={{0,48},{16,0},{32,16},{48,32},{1,49},{17,1},{33,17},{49,33},{2,50}... | collective-permute-start | bytes 393224 | tf_op jit(solution)/shard_map/ppermute | solution.py:22
  11.2 2.4 %collective-permute-start.4 = (f32[8,4096]{1,0:T(8,128)}, f32[8,4096]{1,0:T(8,128)S(1)}, u32[]{:S(2)}, u32[]{:S(2)}) collective-permute-start(f32[8,4096]{1,0:T(8,128)} %param.5), channel_id=1, source_target_pairs={{0,16},{16,32},{32,48},{48,0},{1,17},{17,33},{33,49},{49,1},{2,18}... | collective-permute-start | bytes 393224 | tf_op jit(solution)/shard_map/ppermute | solution.py:22
  14.5 1.0 %copy-done.1 = f32[128,2048]{1,0:T(8,128)} copy-done((f32[128,2048]{1,0:T(8,128)}, f32[128,2048]{1,0:T(8,128)S(1)}, u32[]{:S(2)}) %copy-start.1) | copy-done | bytes 1048600
  15.5 5.7 %shard_map.37 = (f32[2,4,64,256]{3,2,1,0:T(8,128)}, bf16[2,2,256,2048]{3,2,1,0:T(8,128)(2,1)}) custom-call(f32[128,2048]{1,0:T(8,128)} %green_ref.1, f32[128,2048]{1,0:T(8,128)} %copy-done.1, f32[4,2,4,2,8,2048]{5,4,3,2,1,0:T(8,128)} %bitcast.8), custom_call_target="tpu_custom_call" | custom-call | tf_op jit(solution)/shard_map/pallas_call | solution.py:108
  21.2 4.6 %all-to-all-start = ((f32[8,64,256]{2,1,0:T(8,128)}), f32[8,64,256]{2,1,0:T(8,128)S(1)}, u32[]{:S(2)}, u32[]{:S(2)}) async-start(f32[8,64,256]{2,1,0:T(8,128)} %bitcast.9), calls=%async_computation | async-start | bytes 1048576 | tf_op jit(solution)/shard_map/all_to_all | solution.py:26
  25.9 3.9 %collective-permute-done.1.green_x_ref = f32[128,2048]{1,0:T(8,128)S(1)} collective-permute-done((f32[128,2048]{1,0:T(8,128)}, f32[128,2048]{1,0:T(8,128)S(1)}, u32[]{:S(2)}, u32[]{:S(2)}) %collective-permute-start.1) | collective-permute-done | bytes 1048608 | tf_op jit(solution)/shard_map/ppermute | solution.py:18
  29.7 3.5 %all-to-all-done = f32[8,64,256]{2,1,0:T(8,128)S(1)} async-done(((f32[8,64,256]{2,1,0:T(8,128)}), f32[8,64,256]{2,1,0:T(8,128)S(1)}, u32[]{:S(2)}, u32[]{:S(2)}) %all-to-all-start) | async-done | bytes 524320 | tf_op jit(solution)/shard_map/all_to_all | solution.py:26
  33.2 3.2 %collective-permute-start.5 = (f32[128,2048]{1,0:T(8,128)S(1)}, f32[128,2048]{1,0:T(8,128)S(1)}, u32[]{:S(2)}, u32[]{:S(2)}) collective-permute-start(f32[128,2048]{1,0:T(8,128)S(1)} %collective-permute-done.1.green_x_ref), channel_id=1, source_target_pairs={{0,64},{64,0},{1,65},{65,1},{2,66},{66,2},{3,67},{67,3},{4,68},{68... | collective-permute-start | bytes 3145736 | tf_op jit(solution)/shard_map/ppermute | solution.py:18
  38.7 2.2 %copy-done = bf16[2,2,256,2048]{3,2,1,0:T(8,128)(2,1)S(1)} copy-done((bf16[2,2,256,2048]{3,2,1,0:T(8,128)(2,1)S(1)}, bf16[2,2,256,2048]{3,2,1,0:T(8,128)(2,1)}, u32[]{:S(2)}) %copy-start) | copy-done | bytes 4194328
  40.9 3.0 %shard_map.38 = f32[2,4,64,256]{3,2,1,0:T(8,128)} custom-call(f32[128,2048]{1,0:T(8,128)S(1)} %collective-permute-done.1.green_x_ref, f32[128,2048]{1,0:T(8,128)S(1)} %collective-permute-done.5.green_xc_ref, bf16[2,2,256,2048]{3,2,1,0:T(8,128)(2,1)S(1)} %copy-done), custom_call_target="tpu_custom_call" | custom-call | tf_op jit(solution)/shard_map/pallas_call | solution.py:129
  43.9 6.0 %collective-permute-done.6.refs_1_ = f32[32,4096]{1,0:T(8,128)S(1)} collective-permute-done((f32[32,4096]{1,0:T(8,128)S(1)}, f32[32,4096]{1,0:T(8,128)S(1)}, u32[]{:S(2)}, u32[]{:S(2)}) %collective-permute-start.6) | collective-permute-done | bytes 524320 | tf_op jit(solution)/shard_map/ppermute | solution.py:22
  50.0 1.6 %collective-permute-done.7.refs_4_ = f32[32,4096]{1,0:T(8,128)S(1)} collective-permute-done((f32[32,4096]{1,0:T(8,128)S(1)}, f32[32,4096]{1,0:T(8,128)S(1)}, u32[]{:S(2)}, u32[]{:S(2)}) %collective-permute-start.7) | collective-permute-done | bytes 524320 | tf_op jit(solution)/shard_map/ppermute | solution.py:22
  51.6 4.1 %all-to-all-start.1 = ((f32[8,64,256]{2,1,0:T(8,128)}), f32[8,64,256]{2,1,0:T(8,128)}, u32[]{:S(2)}, u32[]{:S(2)}) async-start(f32[8,64,256]{2,1,0:T(8,128)} %bitcast.2), calls=%async_computation.1 | async-start | bytes 1048576 | tf_op jit(solution)/shard_map/all_to_all | solution.py:26
  55.9 2.6 %collective-permute-start.8 = (f32[32,2048]{1,0:T(8,128)S(1)}, f32[32,2048]{1,0:T(8,128)S(1)}, u32[]{:S(2)}, u32[]{:S(2)}) collective-permute-start(f32[32,2048]{1,0:T(8,128)S(1)} %slice.38), channel_id=1, source_target_pairs={{0,6},{2,0},{4,2},{6,4},{1,7},{3,1},{5,3},{7,5},{8,14},{10,8},{12,... | collective-permute-start | bytes 786440 | tf_op jit(solution)/shard_map/ppermute | solution.py:22
  58.6 4.9 %all-to-all-done.1 = f32[8,64,256]{2,1,0:T(8,128)} async-done(((f32[8,64,256]{2,1,0:T(8,128)}), f32[8,64,256]{2,1,0:T(8,128)}, u32[]{:S(2)}, u32[]{:S(2)}) %all-to-all-start.1) | async-done | bytes 524320 | tf_op jit(solution)/shard_map/all_to_all | solution.py:26
  63.5 1.1 %reduce_sum.27 = f32[64,256]{1,0:T(8,128)S(1)} reduce(f32[8,64,256]{2,1,0:T(8,128)} %all-to-all-done.1, f32[]{:T(128)} %constant.13.clone.1), dimensions={0}, to_apply=%region_0.0 | reduce | flops 114688 | bytes 589828 | tf_op jit(solution)/shard_map/reduce_sum | solution.py:174
  65.3 3.7 %all-to-all-start.2 = ((f32[8,32,128]{2,1,0:T(8,128)}), f32[8,32,128]{2,1,0:T(8,128)S(1)}, u32[]{:S(2)}, u32[]{:S(2)}) async-start(f32[8,32,128]{2,1,0:T(8,128)} %bitcast.7), calls=%async_computation.2 | async-start | bytes 262144 | tf_op jit(solution)/shard_map/all_to_all | solution.py:26
  69.0 1.9 %collective-permute-done.9.refs_3_ = f32[32,2048]{1,0:T(8,128)S(1)} collective-permute-done((f32[32,2048]{1,0:T(8,128)S(1)}, f32[32,2048]{1,0:T(8,128)S(1)}, u32[]{:S(2)}, u32[]{:S(2)}) %collective-permute-start.9) | collective-permute-done | bytes 262176 | tf_op jit(solution)/shard_map/ppermute | solution.py:22
  70.9 5.7 %all-to-all-done.2.effective_ref = f32[8,32,128]{2,1,0:T(8,128)S(1)} async-done(((f32[8,32,128]{2,1,0:T(8,128)}), f32[8,32,128]{2,1,0:T(8,128)S(1)}, u32[]{:S(2)}, u32[]{:S(2)}) %all-to-all-start.2) | async-done | bytes 131104 | tf_op jit(solution)/shard_map/all_to_all | solution.py:26
  77.3 4.8 %collective-permute-start.10 = (f32[8,8,1024]{2,1,0:T(8,128)S(1)}, f32[8,8,1024]{2,1,0:T(8,128)S(1)}, u32[]{:S(2)}, u32[]{:S(2)}) collective-permute-start(f32[8,8,1024]{2,1,0:T(8,128)S(1)} %get-tuple-element.24), channel_id=1, source_target_pairs={{0,64},{64,0},{1,65},{65,1},{2,66},{66,2},{3,67},{67,3},{4,68},{68... | collective-permute-start | bytes 786440 | tf_op jit(solution)/shard_map/ppermute | solution.py:18
  82.1 1.2 %collective-permute-done.10 = f32[8,8,1024]{2,1,0:T(8,128)S(1)} collective-permute-done((f32[8,8,1024]{2,1,0:T(8,128)S(1)}, f32[8,8,1024]{2,1,0:T(8,128)S(1)}, u32[]{:S(2)}, u32[]{:S(2)}) %collective-permute-start.10) | collective-permute-done | bytes 262176 | tf_op jit(solution)/shard_map/ppermute | solution.py:18
  83.3 10.5 %all_to_all.20 = f32[8,8,1024]{2,1,0:T(8,128)S(1)} all-to-all(f32[8,8,1024]{2,1,0:T(8,128)S(1)} %add.3), channel_id=1, replica_groups=mesh['xh'=2,'c'=2,'zh'=4,'z0'=2,'y'=4,'xl'=2] {'xh','z0','xl'}, dimensions={0} | all-to-all | bytes 524288 | tf_op jit(solution)/shard_map/all_to_all | solution.py:26
  (27 shorter events, 6.4 us)
Async XLA Ops:
  0.0 14.5 %collective-permute-start = (f32[128,2048]{1,0:T(8,128)}, f32[128,2048]{1,0:T(8,128)S(1)}, u32[]{:S(2)}, u32[]{:S(2)}) collective-permute-start(f32[128,2048]{1,0:T(8,128)} %green_ref.1), channel_id=1, source_target_pairs={{0,64},{64,0},{1,65},{65,1},{2,66},{66,2},{3,67},{67,3},{4,68},{68... | collective-permute-start | bytes 3145736 | tf_op jit(solution)/shard_map/ppermute | solution.py:18
  3.2 26.5 %collective-permute-start.1 = (f32[128,2048]{1,0:T(8,128)}, f32[128,2048]{1,0:T(8,128)S(1)}, u32[]{:S(2)}, u32[]{:S(2)}) collective-permute-start(f32[128,2048]{1,0:T(8,128)} %green_ref.1), channel_id=1, source_target_pairs={{0,128},{128,0},{1,129},{129,1},{2,130},{130,2},{3,131},{131,3},{4... | collective-permute-start | bytes 3145736 | tf_op jit(solution)/shard_map/ppermute | solution.py:18
  4.2 21.6 %collective-permute-start.2 = (f32[8,4096]{1,0:T(8,128)}, f32[8,4096]{1,0:T(8,128)S(1)}, u32[]{:S(2)}, u32[]{:S(2)}) collective-permute-start(f32[8,4096]{1,0:T(8,128)} %param.5), channel_id=1, source_target_pairs={{0,48},{16,0},{32,16},{48,32},{1,49},{17,1},{33,17},{49,33},{2,50}... | collective-permute-start | bytes 393224 | tf_op jit(solution)/shard_map/ppermute | solution.py:22
  10.3 15.6 %collective-permute-start.3 = (f32[8,4096]{1,0:T(8,128)}, f32[8,4096]{1,0:T(8,128)S(1)}, u32[]{:S(2)}, u32[]{:S(2)}) collective-permute-start(f32[8,4096]{1,0:T(8,128)} %param.5), channel_id=1, source_target_pairs={{0,32},{16,48},{32,0},{48,16},{1,33},{17,49},{33,1},{49,17},{2,34}... | collective-permute-start | bytes 393224 | tf_op jit(solution)/shard_map/ppermute | solution.py:22
  11.2 14.7 %collective-permute-start.4 = (f32[8,4096]{1,0:T(8,128)}, f32[8,4096]{1,0:T(8,128)S(1)}, u32[]{:S(2)}, u32[]{:S(2)}) collective-permute-start(f32[8,4096]{1,0:T(8,128)} %param.5), channel_id=1, source_target_pairs={{0,16},{16,32},{32,48},{48,0},{1,17},{17,33},{33,49},{49,1},{2,18}... | collective-permute-start | bytes 393224 | tf_op jit(solution)/shard_map/ppermute | solution.py:22
  14.5 1.0 %copy-start.1 = (f32[128,2048]{1,0:T(8,128)}, f32[128,2048]{1,0:T(8,128)S(1)}, u32[]{:S(2)}) copy-start(f32[128,2048]{1,0:T(8,128)S(1)} %collective-permute-done.green_c_ref) | copy-start | bytes 3145732
  21.2 12.0 %all-to-all-start = ((f32[8,64,256]{2,1,0:T(8,128)}), f32[8,64,256]{2,1,0:T(8,128)S(1)}, u32[]{:S(2)}, u32[]{:S(2)}) async-start(f32[8,64,256]{2,1,0:T(8,128)} %bitcast.9), calls=%async_computation | async-start | bytes 1048576 | tf_op jit(solution)/shard_map/all_to_all | solution.py:26
  33.2 5.5 %collective-permute-start.5 = (f32[128,2048]{1,0:T(8,128)S(1)}, f32[128,2048]{1,0:T(8,128)S(1)}, u32[]{:S(2)}, u32[]{:S(2)}) collective-permute-start(f32[128,2048]{1,0:T(8,128)S(1)} %collective-permute-done.1.green_x_ref), channel_id=1, source_target_pairs={{0,64},{64,0},{1,65},{65,1},{2,66},{66,2},{3,67},{67,3},{4,68},{68... | collective-permute-start | bytes 3145736 | tf_op jit(solution)/shard_map/ppermute | solution.py:18
  36.4 13.6 %collective-permute-start.6 = (f32[32,4096]{1,0:T(8,128)S(1)}, f32[32,4096]{1,0:T(8,128)S(1)}, u32[]{:S(2)}, u32[]{:S(2)}) collective-permute-start(f32[32,4096]{1,0:T(8,128)S(1)} %constant_dynamic-update-slice_fusion.refs_0_), channel_id=1, source_target_pairs={{0,6},{2,0},{4,2},{6,4},{1,7},{3,1},{5,3},{7,5},{8,14},{10,8},{12,... | collective-permute-start | bytes 1572872 | tf_op jit(solution)/shard_map/ppermute | solution.py:22
  37.2 14.4 %collective-permute-start.7 = (f32[32,4096]{1,0:T(8,128)S(1)}, f32[32,4096]{1,0:T(8,128)S(1)}, u32[]{:S(2)}, u32[]{:S(2)}) collective-permute-start(f32[32,4096]{1,0:T(8,128)S(1)} %constant_dynamic-update-slice_fusion.refs_0_), channel_id=1, source_target_pairs={{0,2},{2,4},{4,6},{6,0},{1,3},{3,5},{5,7},{7,1},{8,10},{10,12},{12... | collective-permute-start | bytes 1572872 | tf_op jit(solution)/shard_map/ppermute | solution.py:22
  38.7 2.2 %copy-start = (bf16[2,2,256,2048]{3,2,1,0:T(8,128)(2,1)S(1)}, bf16[2,2,256,2048]{3,2,1,0:T(8,128)(2,1)}, u32[]{:S(2)}) copy-start(bf16[2,2,256,2048]{3,2,1,0:T(8,128)(2,1)} %get-tuple-element.17.rows_ref) | copy-start | bytes 12582916
  51.6 11.9 %all-to-all-start.1 = ((f32[8,64,256]{2,1,0:T(8,128)}), f32[8,64,256]{2,1,0:T(8,128)}, u32[]{:S(2)}, u32[]{:S(2)}) async-start(f32[8,64,256]{2,1,0:T(8,128)} %bitcast.2), calls=%async_computation.1 | async-start | bytes 1048576 | tf_op jit(solution)/shard_map/all_to_all | solution.py:26
  55.9 13.2 %collective-permute-start.8 = (f32[32,2048]{1,0:T(8,128)S(1)}, f32[32,2048]{1,0:T(8,128)S(1)}, u32[]{:S(2)}, u32[]{:S(2)}) collective-permute-start(f32[32,2048]{1,0:T(8,128)S(1)} %slice.38), channel_id=1, source_target_pairs={{0,6},{2,0},{4,2},{6,4},{1,7},{3,1},{5,3},{7,5},{8,14},{10,8},{12,... | collective-permute-start | bytes 786440 | tf_op jit(solution)/shard_map/ppermute | solution.py:22
  58.5 12.4 %collective-permute-start.9 = (f32[32,2048]{1,0:T(8,128)S(1)}, f32[32,2048]{1,0:T(8,128)S(1)}, u32[]{:S(2)}, u32[]{:S(2)}) collective-permute-start(f32[32,2048]{1,0:T(8,128)S(1)} %slice.39), channel_id=1, source_target_pairs={{0,2},{2,4},{4,6},{6,0},{1,3},{3,5},{5,7},{7,1},{8,10},{10,12},{12... | collective-permute-start | bytes 786440 | tf_op jit(solution)/shard_map/ppermute | solution.py:22
  65.3 11.3 %all-to-all-start.2 = ((f32[8,32,128]{2,1,0:T(8,128)}), f32[8,32,128]{2,1,0:T(8,128)S(1)}, u32[]{:S(2)}, u32[]{:S(2)}) async-start(f32[8,32,128]{2,1,0:T(8,128)} %bitcast.7), calls=%async_computation.2 | async-start | bytes 262144 | tf_op jit(solution)/shard_map/all_to_all | solution.py:26
  77.3 6.0 %collective-permute-start.10 = (f32[8,8,1024]{2,1,0:T(8,128)S(1)}, f32[8,8,1024]{2,1,0:T(8,128)S(1)}, u32[]{:S(2)}, u32[]{:S(2)}) collective-permute-start(f32[8,8,1024]{2,1,0:T(8,128)S(1)} %get-tuple-element.24), channel_id=1, source_target_pairs={{0,64},{64,0},{1,65},{65,1},{2,66},{66,2},{3,67},{67,3},{4,68},{68... | collective-permute-start | bytes 786440 | tf_op jit(solution)/shard_map/ppermute | solution.py:18

commit v5 on v4

--- a/solution.py
+++ b/solution.py
@@ -167,8 +167,9 @@
     near, green_x, owned = lax.optimization_barrier((near, green_x, owned))
     far = far_terms(green_x, move(green_x, "c"), rows)
     far, up, down = lax.optimization_barrier((far, up, down))
+    far = exchange(far.reshape(8, 64, 256), ("z0", "y"))
+    far, up, down = lax.optimization_barrier((far, up, down))
     left, right = from_above(up[:, :2048], "y", 1), from_above(down[:, 2048:], "y", 3)
-    far = exchange(far.reshape(8, 64, 256), ("z0", "y"))
     factors = [owned, up, left, right, down]
 
     near, far = by_row_part(jnp.sum(near, axis=0)), by_row_part(jnp.sum(far, axis=0))

time: 95 us -> 94.1 us (level)
  blocking collectives: 10.5 us -> 21.6 us
  starting transfers between devices: 38.2 us -> 32.9 us
  waiting for transfers between devices: 29.5 us -> 24.6 us
  other arithmetic: 2.48 us -> 0.78 us
    all_to_all x1 -> x2, blocking collectives: 10.5 us -> 21.6 us  [exchange(): return lax.all_to_all(pieces, axes, 0, 0, tiled=True)]
    all_to_all x3 -> x2, starting transfers between devices: 12.5 us -> 8.14 us  [exchange(): return lax.all_to_all(pieces, axes, 0, 0, tiled=True)]
    all_to_all x3 -> x2, waiting for transfers between devices: 14.1 us -> 11 us  [exchange(): return lax.all_to_all(pieces, axes, 0, 0, tiled=True)]
    ppermute x7, waiting for transfers between devices: 9.55 us -> 7.71 us  [from_above(): return lax.ppermute(x, axis, [(i, (i - steps) % 4) for i in range(4)])]
    reduce_sum x1, other arithmetic: 1.08 us -> 0.04 us  [per_device(): jnp.sum(far, axis=0)]
  transfers between devices with their start and end apart: 14 -> 13, of which waited for: 9 -> 7; matrix products, arithmetic and copies ran while one was open for 3% -> 1% of each run, Pallas kernels for 9% -> 9%
where the time goes in v5:
time: 94.1 us; the launch traced here: 93.6 us
  starting transfers between devices  32.9 us (35%)
  waiting for transfers between devices  24.6 us (26%)
  blocking collectives  21.6 us (23%)
  Pallas kernels  9.38 us (10%)
  local copies, waits for them, and re-layouts  4.19 us (4%)
    all_to_all x2, blocking collectives, exchange(): return lax.all_to_all(pieces, axes, 0, 0, tiled=True)  21.6 us
    ppermute x7, starting transfers between devices, from_above(): return lax.ppermute(x, axis, [(i, (i - steps) % 4) for i in range(4)])  12.6 us
    ppermute x4, starting transfers between devices, move(): return lax.ppermute(x, axis, [(0, 1), (1, 0)])  12.2 us
    all_to_all x2, waiting for transfers between devices, exchange(): return lax.all_to_all(pieces, axes, 0, 0, tiled=True)  11 us
    all_to_all x2, starting transfers between devices, exchange(): return lax.all_to_all(pieces, axes, 0, 0, tiled=True)  8.14 us
    ppermute x7, waiting for transfers between devices, from_above(): return lax.ppermute(x, axis, [(i, (i - steps) % 4) for i in range(4)])  7.71 us
    ppermute x4, waiting for transfers between devices, move(): return lax.ppermute(x, axis, [(0, 1), (1, 0)])  5.87 us
    pallas_call x1, Pallas kernels, near_terms(): pl.pallas_call(near_kernel, out_shape=(jax.ShapeDtypeStruct((2, 4, 64, 25...  5.68 us
  transfers between devices with their start and end apart: 13, of which 7 were waited for; matrix products, arithmetic and copies ran while one was open for 1% of the time, Pallas kernels for 9%

profile of v5, /device:TPU:1, one launch (start us, length us, event | category | flops | bytes accessed | tf_op | source)
XLA Modules:
  0.0 93.6 jit_solution(2345997838250667651)
XLA Ops:
  0.0 3.2 %collective-permute-start = (f32[128,2048]{1,0:T(8,128)}, f32[128,2048]{1,0:T(8,128)S(1)}, u32[]{:S(2)}, u32[]{:S(2)}) collective-permute-start(f32[128,2048]{1,0:T(8,128)} %green_ref.1), channel_id=1, source_target_pairs={{0,64},{64,0},{1,65},{65,1},{2,66},{66,2},{3,67},{67,3},{4,68},{68... | collective-permute-start | bytes 3145736 | tf_op jit(solution)/shard_map/ppermute | solution.py:18
  3.2 1.0 %collective-permute-start.1 = (f32[128,2048]{1,0:T(8,128)}, f32[128,2048]{1,0:T(8,128)S(1)}, u32[]{:S(2)}, u32[]{:S(2)}) collective-permute-start(f32[128,2048]{1,0:T(8,128)} %green_ref.1), channel_id=1, source_target_pairs={{0,128},{128,0},{1,129},{129,1},{2,130},{130,2},{3,131},{131,3},{4... | collective-permute-start | bytes 3145736 | tf_op jit(solution)/shard_map/ppermute | solution.py:18
  4.2 6.0 %collective-permute-start.2 = (f32[8,4096]{1,0:T(8,128)}, f32[8,4096]{1,0:T(8,128)S(1)}, u32[]{:S(2)}, u32[]{:S(2)}) collective-permute-start(f32[8,4096]{1,0:T(8,128)} %param.5), channel_id=1, source_target_pairs={{0,48},{16,0},{32,16},{48,32},{1,49},{17,1},{33,17},{49,33},{2,50}... | collective-permute-start | bytes 393224 | tf_op jit(solution)/shard_map/ppermute | solution.py:22
  10.3 0.9 collective-permute-start.3
  11.2 2.4 %collective-permute-start.4 = (f32[8,4096]{1,0:T(8,128)}, f32[8,4096]{1,0:T(8,128)S(1)}, u32[]{:S(2)}, u32[]{:S(2)}) collective-permute-start(f32[8,4096]{1,0:T(8,128)} %param.5), channel_id=1, source_target_pairs={{0,16},{16,32},{32,48},{48,0},{1,17},{17,33},{33,49},{49,1},{2,18}... | collective-permute-start | bytes 393224 | tf_op jit(solution)/shard_map/ppermute | solution.py:22
  13.5 0.9 %constant_dynamic-update-slice_fusion.3 = f32[32,4096]{1,0:T(8,128)S(1)} fusion(f32[8,4096]{1,0:T(8,128)} %param.5), kind=kLoop, calls=%fused_computation.5 | loop fusion | bytes 262144
  14.5 1.0 %copy-done.1 = f32[128,2048]{1,0:T(8,128)} copy-done((f32[128,2048]{1,0:T(8,128)}, f32[128,2048]{1,0:T(8,128)S(1)}, u32[]{:S(2)}) %copy-start.1) | copy-done | bytes 1048600
  15.4 5.7 %shard_map.37 = (f32[2,4,64,256]{3,2,1,0:T(8,128)}, bf16[2,2,256,2048]{3,2,1,0:T(8,128)(2,1)}) custom-call(f32[128,2048]{1,0:T(8,128)} %green_ref.1, f32[128,2048]{1,0:T(8,128)} %copy-done.1, f32[4,2,4,2,8,2048]{5,4,3,2,1,0:T(8,128)} %bitcast.8), custom_call_target="tpu_custom_call" | custom-call | tf_op jit(solution)/shard_map/pallas_call | solution.py:108
  21.1 4.6 %all-to-all-start = ((f32[8,64,256]{2,1,0:T(8,128)}), f32[8,64,256]{2,1,0:T(8,128)S(1)}, u32[]{:S(2)}, u32[]{:S(2)}) async-start(f32[8,64,256]{2,1,0:T(8,128)} %bitcast.10), calls=%async_computation | async-start | bytes 1048576 | tf_op jit(solution)/shard_map/all_to_all | solution.py:26
  25.9 3.9 %collective-permute-done.1.green_x_ref = f32[128,2048]{1,0:T(8,128)S(1)} collective-permute-done((f32[128,2048]{1,0:T(8,128)}, f32[128,2048]{1,0:T(8,128)S(1)}, u32[]{:S(2)}, u32[]{:S(2)}) %collective-permute-start.1) | collective-permute-done | bytes 1048608 | tf_op jit(solution)/shard_map/ppermute | solution.py:18
  29.7 3.4 %all-to-all-done = f32[8,64,256]{2,1,0:T(8,128)S(1)} async-done(((f32[8,64,256]{2,1,0:T(8,128)}), f32[8,64,256]{2,1,0:T(8,128)S(1)}, u32[]{:S(2)}, u32[]{:S(2)}) %all-to-all-start) | async-done | bytes 524320 | tf_op jit(solution)/shard_map/all_to_all | solution.py:26
  33.2 3.2 %collective-permute-start.5 = (f32[128,2048]{1,0:T(8,128)S(1)}, f32[128,2048]{1,0:T(8,128)S(1)}, u32[]{:S(2)}, u32[]{:S(2)}) collective-permute-start(f32[128,2048]{1,0:T(8,128)S(1)} %collective-permute-done.1.green_x_ref), channel_id=1, source_target_pairs={{0,64},{64,0},{1,65},{65,1},{2,66},{66,2},{3,67},{67,3},{4,68},{68... | collective-permute-start | bytes 3145736 | tf_op jit(solution)/shard_map/ppermute | solution.py:18
  37.9 0.8 collective-permute-done.5.green_xc_ref
  38.7 2.2 %copy-done = bf16[2,2,256,2048]{3,2,1,0:T(8,128)(2,1)S(1)} copy-done((bf16[2,2,256,2048]{3,2,1,0:T(8,128)(2,1)S(1)}, bf16[2,2,256,2048]{3,2,1,0:T(8,128)(2,1)}, u32[]{:S(2)}) %copy-start) | copy-done | bytes 4194328
  40.9 3.0 %shard_map.38 = f32[2,4,64,256]{3,2,1,0:T(8,128)} custom-call(f32[128,2048]{1,0:T(8,128)S(1)} %collective-permute-done.1.green_x_ref, f32[128,2048]{1,0:T(8,128)S(1)} %collective-permute-done.5.green_xc_ref, bf16[2,2,256,2048]{3,2,1,0:T(8,128)(2,1)S(1)} %copy-done), custom_call_target="tpu_custom_call" | custom-call | tf_op jit(solution)/shard_map/pallas_call | solution.py:129
  43.9 6.1 %collective-permute-done.6.refs_1_ = f32[32,4096]{1,0:T(8,128)S(1)} collective-permute-done((f32[32,4096]{1,0:T(8,128)S(1)}, f32[32,4096]{1,0:T(8,128)S(1)}, u32[]{:S(2)}, u32[]{:S(2)}) %collective-permute-start.6) | collective-permute-done | bytes 524320 | tf_op jit(solution)/shard_map/ppermute | solution.py:22
  50.0 1.6 %collective-permute-done.7.refs_4_ = f32[32,4096]{1,0:T(8,128)S(1)} collective-permute-done((f32[32,4096]{1,0:T(8,128)S(1)}, f32[32,4096]{1,0:T(8,128)S(1)}, u32[]{:S(2)}, u32[]{:S(2)}) %collective-permute-start.7) | collective-permute-done | bytes 524320 | tf_op jit(solution)/shard_map/ppermute | solution.py:22
  51.6 3.5 %all-to-all-start.1 = ((f32[8,64,256]{2,1,0:T(8,128)}), f32[8,64,256]{2,1,0:T(8,128)S(1)}, u32[]{:S(2)}, u32[]{:S(2)}) async-start(f32[8,64,256]{2,1,0:T(8,128)} %bitcast.2), calls=%async_computation.1 | async-start | bytes 1048576 | tf_op jit(solution)/shard_map/all_to_all | solution.py:26
  55.2 7.6 %all-to-all-done.1 = f32[8,64,256]{2,1,0:T(8,128)S(1)} async-done(((f32[8,64,256]{2,1,0:T(8,128)}), f32[8,64,256]{2,1,0:T(8,128)S(1)}, u32[]{:S(2)}, u32[]{:S(2)}) %all-to-all-start.1) | async-done | bytes 524320 | tf_op jit(solution)/shard_map/all_to_all | solution.py:26
  62.8 1.8 %collective-permute-start.8 = (f32[32,2048]{1,0:T(8,128)S(1)}, f32[32,2048]{1,0:T(8,128)S(1)}, u32[]{:S(2)}, u32[]{:S(2)}) collective-permute-start(f32[32,2048]{1,0:T(8,128)S(1)} %slice.38), channel_id=1, source_target_pairs={{0,6},{2,0},{4,2},{6,4},{1,7},{3,1},{5,3},{7,5},{8,14},{10,8},{12,... | collective-permute-start | bytes 786440 | tf_op jit(solution)/shard_map/ppermute | solution.py:22
  64.8 11.1 %all_to_all.20.effective_ref = f32[8,32,128]{2,1,0:T(8,128)S(1)} all-to-all(f32[8,32,128]{2,1,0:T(8,128)S(1)} %bitcast.9), channel_id=1, replica_groups=mesh['xh'=2,'c'=2,'zh'=4,'z0'=2,'y'=4,'xl'=2] {'zh','xl'}, dimensions={0} | all-to-all | bytes 262144 | tf_op jit(solution)/shard_map/all_to_all | solution.py:26
  76.6 4.7 %collective-permute-start.10 = (f32[8,8,1024]{2,1,0:T(8,128)S(1)}, f32[8,8,1024]{2,1,0:T(8,128)S(1)}, u32[]{:S(2)}, u32[]{:S(2)}) collective-permute-start(f32[8,8,1024]{2,1,0:T(8,128)S(1)} %get-tuple-element.30), channel_id=1, source_target_pairs={{0,64},{64,0},{1,65},{65,1},{2,66},{66,2},{3,67},{67,3},{4,68},{68... | collective-permute-start | bytes 786440 | tf_op jit(solution)/shard_map/ppermute | solution.py:18
  81.3 1.2 %collective-permute-done.10 = f32[8,8,1024]{2,1,0:T(8,128)S(1)} collective-permute-done((f32[8,8,1024]{2,1,0:T(8,128)S(1)}, f32[8,8,1024]{2,1,0:T(8,128)S(1)}, u32[]{:S(2)}, u32[]{:S(2)}) %collective-permute-start.10) | collective-permute-done | bytes 262176 | tf_op jit(solution)/shard_map/ppermute | solution.py:18
  82.5 10.5 %all_to_all.21 = f32[8,8,1024]{2,1,0:T(8,128)S(1)} all-to-all(f32[8,8,1024]{2,1,0:T(8,128)S(1)} %add.3), channel_id=1, replica_groups=mesh['xh'=2,'c'=2,'zh'=4,'z0'=2,'y'=4,'xl'=2] {'xh','z0','xl'}, dimensions={0} | all-to-all | bytes 524288 | tf_op jit(solution)/shard_map/all_to_all | solution.py:26
  (26 shorter events, 3.1 us)
Async XLA Ops:
  0.0 14.5 %collective-permute-start = (f32[128,2048]{1,0:T(8,128)}, f32[128,2048]{1,0:T(8,128)S(1)}, u32[]{:S(2)}, u32[]{:S(2)}) collective-permute-start(f32[128,2048]{1,0:T(8,128)} %green_ref.1), channel_id=1, source_target_pairs={{0,64},{64,0},{1,65},{65,1},{2,66},{66,2},{3,67},{67,3},{4,68},{68... | collective-permute-start | bytes 3145736 | tf_op jit(solution)/shard_map/ppermute | solution.py:18
  3.2 26.5 %collective-permute-start.1 = (f32[128,2048]{1,0:T(8,128)}, f32[128,2048]{1,0:T(8,128)S(1)}, u32[]{:S(2)}, u32[]{:S(2)}) collective-permute-start(f32[128,2048]{1,0:T(8,128)} %green_ref.1), channel_id=1, source_target_pairs={{0,128},{128,0},{1,129},{129,1},{2,130},{130,2},{3,131},{131,3},{4... | collective-permute-start | bytes 3145736 | tf_op jit(solution)/shard_map/ppermute | solution.py:18
  4.2 21.5 %collective-permute-start.2 = (f32[8,4096]{1,0:T(8,128)}, f32[8,4096]{1,0:T(8,128)S(1)}, u32[]{:S(2)}, u32[]{:S(2)}) collective-permute-start(f32[8,4096]{1,0:T(8,128)} %param.5), channel_id=1, source_target_pairs={{0,48},{16,0},{32,16},{48,32},{1,49},{17,1},{33,17},{49,33},{2,50}... | collective-permute-start | bytes 393224 | tf_op jit(solution)/shard_map/ppermute | solution.py:22
  10.3 15.5 %collective-permute-start.3 = (f32[8,4096]{1,0:T(8,128)}, f32[8,4096]{1,0:T(8,128)S(1)}, u32[]{:S(2)}, u32[]{:S(2)}) collective-permute-start(f32[8,4096]{1,0:T(8,128)} %param.5), channel_id=1, source_target_pairs={{0,32},{16,48},{32,0},{48,16},{1,33},{17,49},{33,1},{49,17},{2,34}... | collective-permute-start | bytes 393224 | tf_op jit(solution)/shard_map/ppermute | solution.py:22
  11.2 14.7 %collective-permute-start.4 = (f32[8,4096]{1,0:T(8,128)}, f32[8,4096]{1,0:T(8,128)S(1)}, u32[]{:S(2)}, u32[]{:S(2)}) collective-permute-start(f32[8,4096]{1,0:T(8,128)} %param.5), channel_id=1, source_target_pairs={{0,16},{16,32},{32,48},{48,0},{1,17},{17,33},{33,49},{49,1},{2,18}... | collective-permute-start | bytes 393224 | tf_op jit(solution)/shard_map/ppermute | solution.py:22
  14.5 1.0 %copy-start.1 = (f32[128,2048]{1,0:T(8,128)}, f32[128,2048]{1,0:T(8,128)S(1)}, u32[]{:S(2)}) copy-start(f32[128,2048]{1,0:T(8,128)S(1)} %collective-permute-done.green_c_ref) | copy-start | bytes 3145732
  21.1 12.0 %all-to-all-start = ((f32[8,64,256]{2,1,0:T(8,128)}), f32[8,64,256]{2,1,0:T(8,128)S(1)}, u32[]{:S(2)}, u32[]{:S(2)}) async-start(f32[8,64,256]{2,1,0:T(8,128)} %bitcast.10), calls=%async_computation | async-start | bytes 1048576 | tf_op jit(solution)/shard_map/all_to_all | solution.py:26
  33.2 5.5 %collective-permute-start.5 = (f32[128,2048]{1,0:T(8,128)S(1)}, f32[128,2048]{1,0:T(8,128)S(1)}, u32[]{:S(2)}, u32[]{:S(2)}) collective-permute-start(f32[128,2048]{1,0:T(8,128)S(1)} %collective-permute-done.1.green_x_ref), channel_id=1, source_target_pairs={{0,64},{64,0},{1,65},{65,1},{2,66},{66,2},{3,67},{67,3},{4,68},{68... | collective-permute-start | bytes 3145736 | tf_op jit(solution)/shard_map/ppermute | solution.py:18
  36.4 13.6 %collective-permute-start.6 = (f32[32,4096]{1,0:T(8,128)S(1)}, f32[32,4096]{1,0:T(8,128)S(1)}, u32[]{:S(2)}, u32[]{:S(2)}) collective-permute-start(f32[32,4096]{1,0:T(8,128)S(1)} %constant_dynamic-update-slice_fusion.refs_0_), channel_id=1, source_target_pairs={{0,6},{2,0},{4,2},{6,4},{1,7},{3,1},{5,3},{7,5},{8,14},{10,8},{12,... | collective-permute-start | bytes 1572872 | tf_op jit(solution)/shard_map/ppermute | solution.py:22
  37.1 14.4 %collective-permute-start.7 = (f32[32,4096]{1,0:T(8,128)S(1)}, f32[32,4096]{1,0:T(8,128)S(1)}, u32[]{:S(2)}, u32[]{:S(2)}) collective-permute-start(f32[32,4096]{1,0:T(8,128)S(1)} %constant_dynamic-update-slice_fusion.refs_0_), channel_id=1, source_target_pairs={{0,2},{2,4},{4,6},{6,0},{1,3},{3,5},{5,7},{7,1},{8,10},{10,12},{12... | collective-permute-start | bytes 1572872 | tf_op jit(solution)/shard_map/ppermute | solution.py:22
  38.7 2.2 %copy-start = (bf16[2,2,256,2048]{3,2,1,0:T(8,128)(2,1)S(1)}, bf16[2,2,256,2048]{3,2,1,0:T(8,128)(2,1)}, u32[]{:S(2)}) copy-start(bf16[2,2,256,2048]{3,2,1,0:T(8,128)(2,1)} %get-tuple-element.20.rows_ref) | copy-start | bytes 12582916
  51.6 11.1 %all-to-all-start.1 = ((f32[8,64,256]{2,1,0:T(8,128)}), f32[8,64,256]{2,1,0:T(8,128)S(1)}, u32[]{:S(2)}, u32[]{:S(2)}) async-start(f32[8,64,256]{2,1,0:T(8,128)} %bitcast.2), calls=%async_computation.1 | async-start | bytes 1048576 | tf_op jit(solution)/shard_map/all_to_all | solution.py:26
  62.8 13.0 %collective-permute-start.8 = (f32[32,2048]{1,0:T(8,128)S(1)}, f32[32,2048]{1,0:T(8,128)S(1)}, u32[]{:S(2)}, u32[]{:S(2)}) collective-permute-start(f32[32,2048]{1,0:T(8,128)S(1)} %slice.38), channel_id=1, source_target_pairs={{0,6},{2,0},{4,2},{6,4},{1,7},{3,1},{5,3},{7,5},{8,14},{10,8},{12,... | collective-permute-start | bytes 786440 | tf_op jit(solution)/shard_map/ppermute | solution.py:22
  64.6 11.3 %collective-permute-start.9 = (f32[32,2048]{1,0:T(8,128)S(1)}, f32[32,2048]{1,0:T(8,128)S(1)}, u32[]{:S(2)}, u32[]{:S(2)}) collective-permute-start(f32[32,2048]{1,0:T(8,128)S(1)} %slice.39), channel_id=1, source_target_pairs={{0,2},{2,4},{4,6},{6,0},{1,3},{3,5},{5,7},{7,1},{8,10},{10,12},{12... | collective-permute-start | bytes 786440 | tf_op jit(solution)/shard_map/ppermute | solution.py:22
  76.6 5.9 %collective-permute-start.10 = (f32[8,8,1024]{2,1,0:T(8,128)S(1)}, f32[8,8,1024]{2,1,0:T(8,128)S(1)}, u32[]{:S(2)}, u32[]{:S(2)}) collective-permute-start(f32[8,8,1024]{2,1,0:T(8,128)S(1)} %get-tuple-element.30), channel_id=1, source_target_pairs={{0,64},{64,0},{1,65},{65,1},{2,66},{66,2},{3,67},{67,3},{4,68},{68... | collective-permute-start | bytes 786440 | tf_op jit(solution)/shard_map/ppermute | solution.py:18

commit v6 on v5

--- a/solution.py
+++ b/solution.py
@@ -86,8 +86,8 @@
         pltpu.roll(effective, 32 - shift, 1),
     )
     high, low = halves(effective)
-    own, up, left, right, down = [halves(ref[...]) for ref in factor_refs]
-    across = [jnp.concatenate(pair, axis=1) for pair in zip(left, right)]
+    own, up, *across, down = [halves(ref[...]) for ref in factor_refs]
+    across = [jnp.concatenate(quarters, axis=1) for quarters in zip(*across)]
     parts = [own, up, across, down]
     both = dot(jnp.concatenate([high, low]), jnp.concatenate([part[0] for part in parts]), ((1,), (0,)))
     cross = dot(high, jnp.concatenate([part[1] for part in parts]), ((1,), (0,)))
@@ -169,8 +169,9 @@
     far, up, down = lax.optimization_barrier((far, up, down))
     far = exchange(far.reshape(8, 64, 256), ("z0", "y"))
     far, up, down = lax.optimization_barrier((far, up, down))
-    left, right = from_above(up[:, :2048], "y", 1), from_above(down[:, 2048:], "y", 3)
-    factors = [owned, up, left, right, down]
+    across = [from_above(up[:, 1024 * k : 1024 * k + 1024], "y", 1) for k in (0, 1)]
+    across += [from_above(down[:, 1024 * k : 1024 * k + 1024], "y", 3) for k in (2, 3)]
+    factors = [owned, up, *across, down]
 
     near, far = by_row_part(jnp.sum(near, axis=0)), by_row_part(jnp.sum(far, axis=0))
     blocks = jnp.concatenate([near, far])

time: 94.1 us -> 94.7 us (level)
  blocking collectives: 21.6 us -> 11.7 us
  waiting for transfers between devices: 24.6 us -> 30.2 us
  starting transfers between devices: 32.9 us -> 37.3 us
    all_to_all x2 -> x1, blocking collectives: 21.6 us -> 11.7 us  [exchange(): return lax.all_to_all(pieces, axes, 0, 0, tiled=True)]
    ppermute x7 -> x9, waiting for transfers between devices: 7.71 us -> 13.3 us  [from_above(): return lax.ppermute(x, axis, [(i, (i - steps) % 4) for i in range(4)])]
    all_to_all x2 -> x3, starting transfers between devices: 8.14 us -> 11.8 us  [exchange(): return lax.all_to_all(pieces, axes, 0, 0, tiled=True)]
    ppermute x7 -> x9, starting transfers between devices: 12.6 us -> 14.1 us  [from_above(): return lax.ppermute(x, axis, [(i, (i - steps) % 4) for i in range(4)])]
    all_to_all x2 -> x3, waiting for transfers between devices: 11 us -> 11 us  [exchange(): return lax.all_to_all(pieces, axes, 0, 0, tiled=True)]
  transfers between devices with their start and end apart: 13 -> 16, of which waited for: 7 -> 11; matrix products, arithmetic and copies ran while one was open for 1% -> 1% of each run, Pallas kernels for 9% -> 9%
where the time goes in v6:
time: 94.7 us; the launch traced here: 94.3 us
  starting transfers between devices  37.3 us (39%)
  waiting for transfers between devices  30.2 us (32%)
  blocking collectives  11.7 us (12%)
  Pallas kernels  9.41 us (10%)
  local copies, waits for them, and re-layouts  4.19 us (4%)
  other arithmetic  1.43 us (2%)
    ppermute x9, starting transfers between devices, from_above(): return lax.ppermute(x, axis, [(i, (i - steps) % 4) for i in range(4)])  14.1 us
    ppermute x9, waiting for transfers between devices, from_above(): return lax.ppermute(x, axis, [(i, (i - steps) % 4) for i in range(4)])  13.3 us
    all_to_all x3, starting transfers between devices, exchange(): return lax.all_to_all(pieces, axes, 0, 0, tiled=True)  11.8 us
    all_to_all x1, blocking collectives, exchange(): return lax.all_to_all(pieces, axes, 0, 0, tiled=True)  11.7 us
    ppermute x4, starting transfers between devices, move(): return lax.ppermute(x, axis, [(0, 1), (1, 0)])  11.3 us
    all_to_all x3, waiting for transfers between devices, exchange(): return lax.all_to_all(pieces, axes, 0, 0, tiled=True)  11 us
    ppermute x4, waiting for transfers between devices, move(): return lax.ppermute(x, axis, [(0, 1), (1, 0)])  5.84 us
    pallas_call x1, Pallas kernels, near_terms(): pl.pallas_call(near_kernel, out_shape=(jax.ShapeDtypeStruct((2, 4, 64, 25...  5.71 us
  transfers between devices with their start and end apart: 16, of which 11 were waited for; matrix products, arithmetic and copies ran while one was open for 1% of the time, Pallas kernels for 9%

profile of v6, /device:TPU:1, one launch (start us, length us, event | category | flops | bytes accessed | tf_op | source)
XLA Modules:
  0.0 94.3 jit_solution(14182628084617390580)
XLA Ops:
  0.0 3.2 %collective-permute-start = (f32[128,2048]{1,0:T(8,128)}, f32[128,2048]{1,0:T(8,128)S(1)}, u32[]{:S(2)}, u32[]{:S(2)}) collective-permute-start(f32[128,2048]{1,0:T(8,128)} %green_ref.1), channel_id=1, source_target_pairs={{0,64},{64,0},{1,65},{65,1},{2,66},{66,2},{3,67},{67,3},{4,68},{68... | collective-permute-start | bytes 3145736 | tf_op jit(solution)/shard_map/ppermute | solution.py:18
  3.2 1.0 %collective-permute-start.1 = (f32[128,2048]{1,0:T(8,128)}, f32[128,2048]{1,0:T(8,128)S(1)}, u32[]{:S(2)}, u32[]{:S(2)}) collective-permute-start(f32[128,2048]{1,0:T(8,128)} %green_ref.1), channel_id=1, source_target_pairs={{0,128},{128,0},{1,129},{129,1},{2,130},{130,2},{3,131},{131,3},{4... | collective-permute-start | bytes 3145736 | tf_op jit(solution)/shard_map/ppermute | solution.py:18
  4.2 6.0 %collective-permute-start.2 = (f32[8,4096]{1,0:T(8,128)}, f32[8,4096]{1,0:T(8,128)S(1)}, u32[]{:S(2)}, u32[]{:S(2)}) collective-permute-start(f32[8,4096]{1,0:T(8,128)} %param.5), channel_id=1, source_target_pairs={{0,48},{16,0},{32,16},{48,32},{1,49},{17,1},{33,17},{49,33},{2,50}... | collective-permute-start | bytes 393224 | tf_op jit(solution)/shard_map/ppermute | solution.py:22
  11.2 2.4 %collective-permute-start.4 = (f32[8,4096]{1,0:T(8,128)}, f32[8,4096]{1,0:T(8,128)S(1)}, u32[]{:S(2)}, u32[]{:S(2)}) collective-permute-start(f32[8,4096]{1,0:T(8,128)} %param.5), channel_id=1, source_target_pairs={{0,16},{16,32},{32,48},{48,0},{1,17},{17,33},{33,49},{49,1},{2,18}... | collective-permute-start | bytes 393224 | tf_op jit(solution)/shard_map/ppermute | solution.py:22
  15.5 5.7 %shard_map.37 = (f32[2,4,64,256]{3,2,1,0:T(8,128)}, bf16[2,2,256,2048]{3,2,1,0:T(8,128)(2,1)}) custom-call(f32[128,2048]{1,0:T(8,128)} %green_ref.1, f32[128,2048]{1,0:T(8,128)} %copy-done.1, f32[4,2,4,2,8,2048]{5,4,3,2,1,0:T(8,128)} %bitcast.8), custom_call_target="tpu_custom_call" | custom-call | tf_op jit(solution)/shard_map/pallas_call | solution.py:108
  21.2 4.6 %all-to-all-start = ((f32[8,64,256]{2,1,0:T(8,128)}), f32[8,64,256]{2,1,0:T(8,128)S(1)}, u32[]{:S(2)}, u32[]{:S(2)}) async-start(f32[8,64,256]{2,1,0:T(8,128)} %bitcast.9), calls=%async_computation | async-start | bytes 1048576 | tf_op jit(solution)/shard_map/all_to_all | solution.py:26
  25.9 3.9 %collective-permute-done.1.green_x_ref = f32[128,2048]{1,0:T(8,128)S(1)} collective-permute-done((f32[128,2048]{1,0:T(8,128)}, f32[128,2048]{1,0:T(8,128)S(1)}, u32[]{:S(2)}, u32[]{:S(2)}) %collective-permute-start.1) | collective-permute-done | bytes 1048608 | tf_op jit(solution)/shard_map/ppermute | solution.py:18
  29.7 3.5 %all-to-all-done = f32[8,64,256]{2,1,0:T(8,128)S(1)} async-done(((f32[8,64,256]{2,1,0:T(8,128)}), f32[8,64,256]{2,1,0:T(8,128)S(1)}, u32[]{:S(2)}, u32[]{:S(2)}) %all-to-all-start) | async-done | bytes 524320 | tf_op jit(solution)/shard_map/all_to_all | solution.py:26
  33.2 3.2 %collective-permute-start.5 = (f32[128,2048]{1,0:T(8,128)S(1)}, f32[128,2048]{1,0:T(8,128)S(1)}, u32[]{:S(2)}, u32[]{:S(2)}) collective-permute-start(f32[128,2048]{1,0:T(8,128)S(1)} %collective-permute-done.1.green_x_ref), channel_id=1, source_target_pairs={{0,64},{64,0},{1,65},{65,1},{2,66},{66,2},{3,67},{67,3},{4,68},{68... | collective-permute-start | bytes 3145736 | tf_op jit(solution)/shard_map/ppermute | solution.py:18
  38.7 2.2 %copy-done = bf16[2,2,256,2048]{3,2,1,0:T(8,128)(2,1)S(1)} copy-done((bf16[2,2,256,2048]{3,2,1,0:T(8,128)(2,1)S(1)}, bf16[2,2,256,2048]{3,2,1,0:T(8,128)(2,1)}, u32[]{:S(2)}) %copy-start) | copy-done | bytes 4194328
  40.9 3.0 %shard_map.38 = f32[2,4,64,256]{3,2,1,0:T(8,128)} custom-call(f32[128,2048]{1,0:T(8,128)S(1)} %collective-permute-done.1.green_x_ref, f32[128,2048]{1,0:T(8,128)S(1)} %collective-permute-done.5.green_xc_ref, bf16[2,2,256,2048]{3,2,1,0:T(8,128)(2,1)S(1)} %copy-done), custom_call_target="tpu_custom_call" | custom-call | tf_op jit(solution)/shard_map/pallas_call | solution.py:129
  43.9 6.1 %collective-permute-done.6.refs_1_ = f32[32,4096]{1,0:T(8,128)S(1)} collective-permute-done((f32[32,4096]{1,0:T(8,128)S(1)}, f32[32,4096]{1,0:T(8,128)S(1)}, u32[]{:S(2)}, u32[]{:S(2)}) %collective-permute-start.6) | collective-permute-done | bytes 524320 | tf_op jit(solution)/shard_map/ppermute | solution.py:22
  50.0 1.6 %collective-permute-done.7.refs_6_ = f32[32,4096]{1,0:T(8,128)S(1)} collective-permute-done((f32[32,4096]{1,0:T(8,128)S(1)}, f32[32,4096]{1,0:T(8,128)S(1)}, u32[]{:S(2)}, u32[]{:S(2)}) %collective-permute-start.7) | collective-permute-done | bytes 524320 | tf_op jit(solution)/shard_map/ppermute | solution.py:22
  51.6 3.5 %all-to-all-start.1 = ((f32[8,64,256]{2,1,0:T(8,128)}), f32[8,64,256]{2,1,0:T(8,128)S(1)}, u32[]{:S(2)}, u32[]{:S(2)}) async-start(f32[8,64,256]{2,1,0:T(8,128)} %bitcast.2), calls=%async_computation.1 | async-start | bytes 1048576 | tf_op jit(solution)/shard_map/all_to_all | solution.py:26
  55.2 7.6 %all-to-all-done.1 = f32[8,64,256]{2,1,0:T(8,128)S(1)} async-done(((f32[8,64,256]{2,1,0:T(8,128)}), f32[8,64,256]{2,1,0:T(8,128)S(1)}, u32[]{:S(2)}, u32[]{:S(2)}) %all-to-all-start.1) | async-done | bytes 524320 | tf_op jit(solution)/shard_map/all_to_all | solution.py:26
  63.5 3.7 %all-to-all-start.2 = ((f32[8,32,128]{2,1,0:T(8,128)}), f32[8,32,128]{2,1,0:T(8,128)S(1)}, u32[]{:S(2)}, u32[]{:S(2)}) async-start(f32[8,32,128]{2,1,0:T(8,128)} %bitcast.7), calls=%async_computation.2 | async-start | bytes 262144 | tf_op jit(solution)/shard_map/all_to_all | solution.py:26
  67.3 1.8 %collective-permute-start.8 = (f32[32,1024]{1,0:T(8,128)S(1)}, f32[32,1024]{1,0:T(8,128)S(1)}, u32[]{:S(2)}, u32[]{:S(2)}) collective-permute-start(f32[32,1024]{1,0:T(8,128)S(1)} %get-tuple-element.34), channel_id=1, source_target_pairs={{0,6},{2,0},{4,2},{6,4},{1,7},{3,1},{5,3},{7,5},{8,14},{10,8},{12,... | collective-permute-start | bytes 393224 | tf_op jit(solution)/shard_map/ppermute | solution.py:22
  69.5 1.1 %collective-permute-start.10 = (f32[32,1024]{1,0:T(8,128)S(1)}, f32[32,1024]{1,0:T(8,128)S(1)}, u32[]{:S(2)}, u32[]{:S(2)}) collective-permute-start(f32[32,1024]{1,0:T(8,128)S(1)} %get-tuple-element.32), channel_id=1, source_target_pairs={{0,2},{2,4},{4,6},{6,0},{1,3},{3,5},{5,7},{7,1},{8,10},{10,12},{12... | collective-permute-start | bytes 393224 | tf_op jit(solution)/shard_map/ppermute | solution.py:22
  71.2 1.7 %collective-permute-done.9.refs_3_ = f32[32,1024]{1,0:T(8,128)S(1)} collective-permute-done((f32[32,1024]{1,0:T(8,128)S(1)}, f32[32,1024]{1,0:T(8,128)S(1)}, u32[]{:S(2)}, u32[]{:S(2)}) %collective-permute-start.9) | collective-permute-done | bytes 131104 | tf_op jit(solution)/shard_map/ppermute | solution.py:22
  72.8 1.8 %collective-permute-done.10.refs_4_ = f32[32,1024]{1,0:T(8,128)S(1)} collective-permute-done((f32[32,1024]{1,0:T(8,128)S(1)}, f32[32,1024]{1,0:T(8,128)S(1)}, u32[]{:S(2)}, u32[]{:S(2)}) %collective-permute-start.10) | collective-permute-done | bytes 131104 | tf_op jit(solution)/shard_map/ppermute | solution.py:22
  74.6 1.6 %collective-permute-done.11.refs_5_ = f32[32,1024]{1,0:T(8,128)S(1)} collective-permute-done((f32[32,1024]{1,0:T(8,128)S(1)}, f32[32,1024]{1,0:T(8,128)S(1)}, u32[]{:S(2)}, u32[]{:S(2)}) %collective-permute-start.11) | collective-permute-done | bytes 131104 | tf_op jit(solution)/shard_map/ppermute | solution.py:22
  77.0 3.8 %collective-permute-start.12 = (f32[8,8,1024]{2,1,0:T(8,128)S(1)}, f32[8,8,1024]{2,1,0:T(8,128)S(1)}, u32[]{:S(2)}, u32[]{:S(2)}) collective-permute-start(f32[8,8,1024]{2,1,0:T(8,128)S(1)} %get-tuple-element.30), channel_id=1, source_target_pairs={{0,64},{64,0},{1,65},{65,1},{2,66},{66,2},{3,67},{67,3},{4,68},{68... | collective-permute-start | bytes 786440 | tf_op jit(solution)/shard_map/ppermute | solution.py:18
  80.8 1.2 %collective-permute-done.12 = f32[8,8,1024]{2,1,0:T(8,128)S(1)} collective-permute-done((f32[8,8,1024]{2,1,0:T(8,128)S(1)}, f32[8,8,1024]{2,1,0:T(8,128)S(1)}, u32[]{:S(2)}, u32[]{:S(2)}) %collective-permute-start.12) | collective-permute-done | bytes 262176 | tf_op jit(solution)/shard_map/ppermute | solution.py:18
  82.0 11.7 %all_to_all.20 = f32[8,8,1024]{2,1,0:T(8,128)S(1)} all-to-all(f32[8,8,1024]{2,1,0:T(8,128)S(1)} %add.3), channel_id=1, replica_groups=mesh['xh'=2,'c'=2,'zh'=4,'z0'=2,'y'=4,'xl'=2] {'xh','z0','xl'}, dimensions={0} | all-to-all | bytes 524288 | tf_op jit(solution)/shard_map/all_to_all | solution.py:26
  (31 shorter events, 8.4 us)
Async XLA Ops:
  0.0 14.5 %collective-permute-start = (f32[128,2048]{1,0:T(8,128)}, f32[128,2048]{1,0:T(8,128)S(1)}, u32[]{:S(2)}, u32[]{:S(2)}) collective-permute-start(f32[128,2048]{1,0:T(8,128)} %green_ref.1), channel_id=1, source_target_pairs={{0,64},{64,0},{1,65},{65,1},{2,66},{66,2},{3,67},{67,3},{4,68},{68... | collective-permute-start | bytes 3145736 | tf_op jit(solution)/shard_map/ppermute | solution.py:18
  3.2 26.5 %collective-permute-start.1 = (f32[128,2048]{1,0:T(8,128)}, f32[128,2048]{1,0:T(8,128)S(1)}, u32[]{:S(2)}, u32[]{:S(2)}) collective-permute-start(f32[128,2048]{1,0:T(8,128)} %green_ref.1), channel_id=1, source_target_pairs={{0,128},{128,0},{1,129},{129,1},{2,130},{130,2},{3,131},{131,3},{4... | collective-permute-start | bytes 3145736 | tf_op jit(solution)/shard_map/ppermute | solution.py:18
  4.2 21.6 %collective-permute-start.2 = (f32[8,4096]{1,0:T(8,128)}, f32[8,4096]{1,0:T(8,128)S(1)}, u32[]{:S(2)}, u32[]{:S(2)}) collective-permute-start(f32[8,4096]{1,0:T(8,128)} %param.5), channel_id=1, source_target_pairs={{0,48},{16,0},{32,16},{48,32},{1,49},{17,1},{33,17},{49,33},{2,50}... | collective-permute-start | bytes 393224 | tf_op jit(solution)/shard_map/ppermute | solution.py:22
  10.3 15.6 %collective-permute-start.3 = (f32[8,4096]{1,0:T(8,128)}, f32[8,4096]{1,0:T(8,128)S(1)}, u32[]{:S(2)}, u32[]{:S(2)}) collective-permute-start(f32[8,4096]{1,0:T(8,128)} %param.5), channel_id=1, source_target_pairs={{0,32},{16,48},{32,0},{48,16},{1,33},{17,49},{33,1},{49,17},{2,34}... | collective-permute-start | bytes 393224 | tf_op jit(solution)/shard_map/ppermute | solution.py:22
  11.2 14.7 %collective-permute-start.4 = (f32[8,4096]{1,0:T(8,128)}, f32[8,4096]{1,0:T(8,128)S(1)}, u32[]{:S(2)}, u32[]{:S(2)}) collective-permute-start(f32[8,4096]{1,0:T(8,128)} %param.5), channel_id=1, source_target_pairs={{0,16},{16,32},{32,48},{48,0},{1,17},{17,33},{33,49},{49,1},{2,18}... | collective-permute-start | bytes 393224 | tf_op jit(solution)/shard_map/ppermute | solution.py:22
  14.5 1.0 %copy-start.1 = (f32[128,2048]{1,0:T(8,128)}, f32[128,2048]{1,0:T(8,128)S(1)}, u32[]{:S(2)}) copy-start(f32[128,2048]{1,0:T(8,128)S(1)} %collective-permute-done.green_c_ref) | copy-start | bytes 3145732
  21.2 12.0 %all-to-all-start = ((f32[8,64,256]{2,1,0:T(8,128)}), f32[8,64,256]{2,1,0:T(8,128)S(1)}, u32[]{:S(2)}, u32[]{:S(2)}) async-start(f32[8,64,256]{2,1,0:T(8,128)} %bitcast.9), calls=%async_computation | async-start | bytes 1048576 | tf_op jit(solution)/shard_map/all_to_all | solution.py:26
  33.2 5.5 %collective-permute-start.5 = (f32[128,2048]{1,0:T(8,128)S(1)}, f32[128,2048]{1,0:T(8,128)S(1)}, u32[]{:S(2)}, u32[]{:S(2)}) collective-permute-start(f32[128,2048]{1,0:T(8,128)S(1)} %collective-permute-done.1.green_x_ref), channel_id=1, source_target_pairs={{0,64},{64,0},{1,65},{65,1},{2,66},{66,2},{3,67},{67,3},{4,68},{68... | collective-permute-start | bytes 3145736 | tf_op jit(solution)/shard_map/ppermute | solution.py:18
  36.4 13.6 %collective-permute-start.6 = (f32[32,4096]{1,0:T(8,128)S(1)}, f32[32,4096]{1,0:T(8,128)S(1)}, u32[]{:S(2)}, u32[]{:S(2)}) collective-permute-start(f32[32,4096]{1,0:T(8,128)S(1)} %constant_dynamic-update-slice_fusion.refs_0_), channel_id=1, source_target_pairs={{0,6},{2,0},{4,2},{6,4},{1,7},{3,1},{5,3},{7,5},{8,14},{10,8},{12,... | collective-permute-start | bytes 1572872 | tf_op jit(solution)/shard_map/ppermute | solution.py:22
  37.2 14.4 %collective-permute-start.7 = (f32[32,4096]{1,0:T(8,128)S(1)}, f32[32,4096]{1,0:T(8,128)S(1)}, u32[]{:S(2)}, u32[]{:S(2)}) collective-permute-start(f32[32,4096]{1,0:T(8,128)S(1)} %constant_dynamic-update-slice_fusion.refs_0_), channel_id=1, source_target_pairs={{0,2},{2,4},{4,6},{6,0},{1,3},{3,5},{5,7},{7,1},{8,10},{10,12},{12... | collective-permute-start | bytes 1572872 | tf_op jit(solution)/shard_map/ppermute | solution.py:22
  38.7 2.2 %copy-start = (bf16[2,2,256,2048]{3,2,1,0:T(8,128)(2,1)S(1)}, bf16[2,2,256,2048]{3,2,1,0:T(8,128)(2,1)}, u32[]{:S(2)}) copy-start(bf16[2,2,256,2048]{3,2,1,0:T(8,128)(2,1)} %get-tuple-element.20.rows_ref) | copy-start | bytes 12582916
  51.6 11.1 %all-to-all-start.1 = ((f32[8,64,256]{2,1,0:T(8,128)}), f32[8,64,256]{2,1,0:T(8,128)S(1)}, u32[]{:S(2)}, u32[]{:S(2)}) async-start(f32[8,64,256]{2,1,0:T(8,128)} %bitcast.2), calls=%async_computation.1 | async-start | bytes 1048576 | tf_op jit(solution)/shard_map/all_to_all | solution.py:26
  63.5 12.7 %all-to-all-start.2 = ((f32[8,32,128]{2,1,0:T(8,128)}), f32[8,32,128]{2,1,0:T(8,128)S(1)}, u32[]{:S(2)}, u32[]{:S(2)}) async-start(f32[8,32,128]{2,1,0:T(8,128)} %bitcast.7), calls=%async_computation.2 | async-start | bytes 262144 | tf_op jit(solution)/shard_map/all_to_all | solution.py:26
  67.3 3.9 %collective-permute-start.8 = (f32[32,1024]{1,0:T(8,128)S(1)}, f32[32,1024]{1,0:T(8,128)S(1)}, u32[]{:S(2)}, u32[]{:S(2)}) collective-permute-start(f32[32,1024]{1,0:T(8,128)S(1)} %get-tuple-element.34), channel_id=1, source_target_pairs={{0,6},{2,0},{4,2},{6,4},{1,7},{3,1},{5,3},{7,5},{8,14},{10,8},{12,... | collective-permute-start | bytes 393224 | tf_op jit(solution)/shard_map/ppermute | solution.py:22
  69.0 3.8 %collective-permute-start.9 = (f32[32,1024]{1,0:T(8,128)S(1)}, f32[32,1024]{1,0:T(8,128)S(1)}, u32[]{:S(2)}, u32[]{:S(2)}) collective-permute-start(f32[32,1024]{1,0:T(8,128)S(1)} %get-tuple-element.33), channel_id=1, source_target_pairs={{0,6},{2,0},{4,2},{6,4},{1,7},{3,1},{5,3},{7,5},{8,14},{10,8},{12,... | collective-permute-start | bytes 393224 | tf_op jit(solution)/shard_map/ppermute | solution.py:22
  69.5 5.1 %collective-permute-start.10 = (f32[32,1024]{1,0:T(8,128)S(1)}, f32[32,1024]{1,0:T(8,128)S(1)}, u32[]{:S(2)}, u32[]{:S(2)}) collective-permute-start(f32[32,1024]{1,0:T(8,128)S(1)} %get-tuple-element.32), channel_id=1, source_target_pairs={{0,2},{2,4},{4,6},{6,0},{1,3},{3,5},{5,7},{7,1},{8,10},{10,12},{12... | collective-permute-start | bytes 393224 | tf_op jit(solution)/shard_map/ppermute | solution.py:22
  70.6 5.7 %collective-permute-start.11 = (f32[32,1024]{1,0:T(8,128)S(1)}, f32[32,1024]{1,0:T(8,128)S(1)}, u32[]{:S(2)}, u32[]{:S(2)}) collective-permute-start(f32[32,1024]{1,0:T(8,128)S(1)} %get-tuple-element.31), channel_id=1, source_target_pairs={{0,2},{2,4},{4,6},{6,0},{1,3},{3,5},{5,7},{7,1},{8,10},{10,12},{12... | collective-permute-start | bytes 393224 | tf_op jit(solution)/shard_map/ppermute | solution.py:22
  77.0 5.0 %collective-permute-start.12 = (f32[8,8,1024]{2,1,0:T(8,128)S(1)}, f32[8,8,1024]{2,1,0:T(8,128)S(1)}, u32[]{:S(2)}, u32[]{:S(2)}) collective-permute-start(f32[8,8,1024]{2,1,0:T(8,128)S(1)} %get-tuple-element.30), channel_id=1, source_target_pairs={{0,64},{64,0},{1,65},{65,1},{2,66},{66,2},{3,67},{67,3},{4,68},{68... | collective-permute-start | bytes 786440 | tf_op jit(solution)/shard_map/ppermute | solution.py:18

commit v7 on v5

--- a/solution.py
+++ b/solution.py
@@ -166,7 +166,7 @@
     up, down = from_above(owned, "y", 1), from_above(owned, "y", 3)
     near, green_x, owned = lax.optimization_barrier((near, green_x, owned))
     far = far_terms(green_x, move(green_x, "c"), rows)
-    far, up, down = lax.optimization_barrier((far, up, down))
+    far, up = lax.optimization_barrier((far, up))
     far = exchange(far.reshape(8, 64, 256), ("z0", "y"))
     far, up, down = lax.optimization_barrier((far, up, down))
     left, right = from_above(up[:, :2048], "y", 1), from_above(down[:, 2048:], "y", 3)

time: 94.1 us -> 104 us (1.11)
  waiting for transfers between devices: 24.6 us -> 34.7 us
    ppermute x7, waiting for transfers between devices: 7.71 us -> 24.6 us  [from_above(): return lax.ppermute(x, axis, [(i, (i - steps) % 4) for i in range(4)])]
    all_to_all x2, waiting for transfers between devices: 11 us -> 3.43 us  [exchange(): return lax.all_to_all(pieces, axes, 0, 0, tiled=True)]
    ppermute x4, starting transfers between devices: 12.2 us -> 11 us  [move(): return lax.ppermute(x, axis, [(0, 1), (1, 0)])]
  transfers between devices with their start and end apart: 13 -> 13, of which waited for: 7 -> 6; matrix products, arithmetic and copies ran while one was open for 1% -> 1% of each run, Pallas kernels for 9% -> 8%
where the time goes in v7:
time: 104 us; the launch traced here: 103 us
  waiting for transfers between devices  34.7 us (33%)
  starting transfers between devices  32.8 us (32%)
  blocking collectives  21.5 us (21%)
  Pallas kernels  9.38 us (9%)
  local copies, waits for them, and re-layouts  4.19 us (4%)
    ppermute x7, waiting for transfers between devices, from_above(): return lax.ppermute(x, axis, [(i, (i - steps) % 4) for i in range(4)])  24.6 us
    all_to_all x2, blocking collectives, exchange(): return lax.all_to_all(pieces, axes, 0, 0, tiled=True)  21.5 us
    ppermute x7, starting transfers between devices, from_above(): return lax.ppermute(x, axis, [(i, (i - steps) % 4) for i in range(4)])  13.1 us
    ppermute x4, starting transfers between devices, move(): return lax.ppermute(x, axis, [(0, 1), (1, 0)])  11 us
    all_to_all x2, starting transfers between devices, exchange(): return lax.all_to_all(pieces, axes, 0, 0, tiled=True)  8.72 us
    ppermute x4, waiting for transfers between devices, move(): return lax.ppermute(x, axis, [(0, 1), (1, 0)])  6.6 us
    pallas_call x1, Pallas kernels, near_terms(): pl.pallas_call(near_kernel, out_shape=(jax.ShapeDtypeStruct((2, 4, 64, 25...  5.68 us
    unnamed x7, local copies, waits for them, and re-layouts  4.11 us
  transfers between devices with their start and end apart: 13, of which 6 were waited for; matrix products, arithmetic and copies ran while one was open for 1% of the time, Pallas kernels for 8%

profile of v7, /device:TPU:1, one launch (start us, length us, event | category | flops | bytes accessed | tf_op | source)
XLA Modules:
  0.0 103.5 jit_solution(4250071384901757040)
XLA Ops:
  0.0 3.2 %collective-permute-start = (f32[128,2048]{1,0:T(8,128)}, f32[128,2048]{1,0:T(8,128)S(1)}, u32[]{:S(2)}, u32[]{:S(2)}) collective-permute-start(f32[128,2048]{1,0:T(8,128)} %green_ref.1), channel_id=1, source_target_pairs={{0,64},{64,0},{1,65},{65,1},{2,66},{66,2},{3,67},{67,3},{4,68},{68... | collective-permute-start | bytes 3145736 | tf_op jit(solution)/shard_map/ppermute | solution.py:18
  3.2 1.0 collective-permute-start.1
  4.2 6.0 %collective-permute-start.2 = (f32[8,4096]{1,0:T(8,128)}, f32[8,4096]{1,0:T(8,128)S(1)}, u32[]{:S(2)}, u32[]{:S(2)}) collective-permute-start(f32[8,4096]{1,0:T(8,128)} %param.5), channel_id=1, source_target_pairs={{0,48},{16,0},{32,16},{48,32},{1,49},{17,1},{33,17},{49,33},{2,50}... | collective-permute-start | bytes 393224 | tf_op jit(solution)/shard_map/ppermute | solution.py:22
  10.3 0.9 collective-permute-start.3
  11.2 2.4 %collective-permute-start.4 = (f32[8,4096]{1,0:T(8,128)}, f32[8,4096]{1,0:T(8,128)S(1)}, u32[]{:S(2)}, u32[]{:S(2)}) collective-permute-start(f32[8,4096]{1,0:T(8,128)} %param.5), channel_id=1, source_target_pairs={{0,16},{16,32},{32,48},{48,0},{1,17},{17,33},{33,49},{49,1},{2,18}... | collective-permute-start | bytes 393224 | tf_op jit(solution)/shard_map/ppermute | solution.py:22
  13.5 0.9 constant_dynamic-update-slice_fusion.3
  14.5 1.0 copy-done.1
  15.4 5.7 %shard_map.37 = (f32[2,4,64,256]{3,2,1,0:T(8,128)}, bf16[2,2,256,2048]{3,2,1,0:T(8,128)(2,1)}) custom-call(f32[128,2048]{1,0:T(8,128)} %green_ref.1, f32[128,2048]{1,0:T(8,128)} %copy-done.1, f32[4,2,4,2,8,2048]{5,4,3,2,1,0:T(8,128)} %bitcast.8), custom_call_target="tpu_custom_call" | custom-call | tf_op jit(solution)/shard_map/pallas_call | solution.py:108
  21.1 4.6 %all-to-all-start = ((f32[8,64,256]{2,1,0:T(8,128)}), f32[8,64,256]{2,1,0:T(8,128)S(1)}, u32[]{:S(2)}, u32[]{:S(2)}) async-start(f32[8,64,256]{2,1,0:T(8,128)} %bitcast.10), calls=%async_computation | async-start | bytes 1048576 | tf_op jit(solution)/shard_map/all_to_all | solution.py:26
  25.9 3.9 %collective-permute-done.1.green_x_ref = f32[128,2048]{1,0:T(8,128)S(1)} collective-permute-done((f32[128,2048]{1,0:T(8,128)}, f32[128,2048]{1,0:T(8,128)S(1)}, u32[]{:S(2)}, u32[]{:S(2)}) %collective-permute-start.1) | collective-permute-done | bytes 1048608 | tf_op jit(solution)/shard_map/ppermute | solution.py:18
  29.7 3.4 %all-to-all-done = f32[8,64,256]{2,1,0:T(8,128)S(1)} async-done(((f32[8,64,256]{2,1,0:T(8,128)}), f32[8,64,256]{2,1,0:T(8,128)S(1)}, u32[]{:S(2)}, u32[]{:S(2)}) %all-to-all-start) | async-done | bytes 524320 | tf_op jit(solution)/shard_map/all_to_all | solution.py:26
  33.2 3.2 %collective-permute-start.5 = (f32[128,2048]{1,0:T(8,128)S(1)}, f32[128,2048]{1,0:T(8,128)S(1)}, u32[]{:S(2)}, u32[]{:S(2)}) collective-permute-start(f32[128,2048]{1,0:T(8,128)S(1)} %collective-permute-done.1.green_x_ref), channel_id=1, source_target_pairs={{0,64},{64,0},{1,65},{65,1},{2,66},{66,2},{3,67},{67,3},{4,68},{68... | collective-permute-start | bytes 3145736 | tf_op jit(solution)/shard_map/ppermute | solution.py:18
  37.1 1.5 %collective-permute-done.5.green_xc_ref = f32[128,2048]{1,0:T(8,128)S(1)} collective-permute-done((f32[128,2048]{1,0:T(8,128)S(1)}, f32[128,2048]{1,0:T(8,128)S(1)}, u32[]{:S(2)}, u32[]{:S(2)}) %collective-permute-start.5) | collective-permute-done | bytes 1048608 | tf_op jit(solution)/shard_map/ppermute | solution.py:18
  38.7 2.2 %copy-done = bf16[2,2,256,2048]{3,2,1,0:T(8,128)(2,1)S(1)} copy-done((bf16[2,2,256,2048]{3,2,1,0:T(8,128)(2,1)S(1)}, bf16[2,2,256,2048]{3,2,1,0:T(8,128)(2,1)}, u32[]{:S(2)}) %copy-start) | copy-done | bytes 4194328
  40.9 3.0 %shard_map.38 = f32[2,4,64,256]{3,2,1,0:T(8,128)} custom-call(f32[128,2048]{1,0:T(8,128)S(1)} %collective-permute-done.1.green_x_ref, f32[128,2048]{1,0:T(8,128)S(1)} %collective-permute-done.5.green_xc_ref, bf16[2,2,256,2048]{3,2,1,0:T(8,128)(2,1)S(1)} %copy-done), custom_call_target="tpu_custom_call" | custom-call | tf_op jit(solution)/shard_map/pallas_call | solution.py:129
  43.9 6.1 %collective-permute-done.6.refs_1_ = f32[32,4096]{1,0:T(8,128)S(1)} collective-permute-done((f32[32,4096]{1,0:T(8,128)S(1)}, f32[32,4096]{1,0:T(8,128)S(1)}, u32[]{:S(2)}, u32[]{:S(2)}) %collective-permute-start.6) | collective-permute-done | bytes 524320 | tf_op jit(solution)/shard_map/ppermute | solution.py:22
  50.0 4.1 %all-to-all-start.1 = ((f32[8,64,256]{2,1,0:T(8,128)}), f32[8,64,256]{2,1,0:T(8,128)S(1)}, u32[]{:S(2)}, u32[]{:S(2)}) async-start(f32[8,64,256]{2,1,0:T(8,128)} %bitcast.2), calls=%async_computation.1 | async-start | bytes 1048576 | tf_op jit(solution)/shard_map/all_to_all | solution.py:26
  54.0 1.5 %collective-permute-start.7 = (f32[32,4096]{1,0:T(8,128)S(1)}, f32[32,4096]{1,0:T(8,128)S(1)}, u32[]{:S(2)}, u32[]{:S(2)}) collective-permute-start(f32[32,4096]{1,0:T(8,128)S(1)} %constant_dynamic-update-slice_fusion.refs_0_), channel_id=1, source_target_pairs={{0,2},{2,4},{4,6},{6,0},{1,3},{3,5},{5,7},{7,1},{8,10},{10,12},{12... | collective-permute-start | bytes 1572872 | tf_op jit(solution)/shard_map/ppermute | solution.py:22
  55.5 18.6 %collective-permute-done.7.refs_4_ = f32[32,4096]{1,0:T(8,128)S(1)} collective-permute-done((f32[32,4096]{1,0:T(8,128)S(1)}, f32[32,4096]{1,0:T(8,128)S(1)}, u32[]{:S(2)}, u32[]{:S(2)}) %collective-permute-start.7) | collective-permute-done | bytes 524320 | tf_op jit(solution)/shard_map/ppermute | solution.py:22
  74.4 1.5 %collective-permute-start.9 = (f32[32,2048]{1,0:T(8,128)S(1)}, f32[32,2048]{1,0:T(8,128)S(1)}, u32[]{:S(2)}, u32[]{:S(2)}) collective-permute-start(f32[32,2048]{1,0:T(8,128)S(1)} %slice.39), channel_id=1, source_target_pairs={{0,2},{2,4},{4,6},{6,0},{1,3},{3,5},{5,7},{7,1},{8,10},{10,12},{12... | collective-permute-start | bytes 786440 | tf_op jit(solution)/shard_map/ppermute | solution.py:22
  75.9 11.2 %all_to_all.20.effective_ref = f32[8,32,128]{2,1,0:T(8,128)S(1)} all-to-all(f32[8,32,128]{2,1,0:T(8,128)S(1)} %bitcast.9), channel_id=1, replica_groups=mesh['xh'=2,'c'=2,'zh'=4,'z0'=2,'y'=4,'xl'=2] {'zh','xl'}, dimensions={0} | all-to-all | bytes 262144 | tf_op jit(solution)/shard_map/all_to_all | solution.py:26
  87.8 3.6 %collective-permute-start.10 = (f32[8,8,1024]{2,1,0:T(8,128)S(1)}, f32[8,8,1024]{2,1,0:T(8,128)S(1)}, u32[]{:S(2)}, u32[]{:S(2)}) collective-permute-start(f32[8,8,1024]{2,1,0:T(8,128)S(1)} %get-tuple-element.28), channel_id=1, source_target_pairs={{0,64},{64,0},{1,65},{65,1},{2,66},{66,2},{3,67},{67,3},{4,68},{68... | collective-permute-start | bytes 786440 | tf_op jit(solution)/shard_map/ppermute | solution.py:18
  91.4 1.2 %collective-permute-done.10 = f32[8,8,1024]{2,1,0:T(8,128)S(1)} collective-permute-done((f32[8,8,1024]{2,1,0:T(8,128)S(1)}, f32[8,8,1024]{2,1,0:T(8,128)S(1)}, u32[]{:S(2)}, u32[]{:S(2)}) %collective-permute-start.10) | collective-permute-done | bytes 262176 | tf_op jit(solution)/shard_map/ppermute | solution.py:18
  92.6 10.3 %all_to_all.21 = f32[8,8,1024]{2,1,0:T(8,128)S(1)} all-to-all(f32[8,8,1024]{2,1,0:T(8,128)S(1)} %add.3), channel_id=1, replica_groups=mesh['xh'=2,'c'=2,'zh'=4,'z0'=2,'y'=4,'xl'=2] {'xh','z0','xl'}, dimensions={0} | all-to-all | bytes 524288 | tf_op jit(solution)/shard_map/all_to_all | solution.py:26
  (26 shorter events, 2.4 us)
Async XLA Ops:
  0.0 14.5 %collective-permute-start = (f32[128,2048]{1,0:T(8,128)}, f32[128,2048]{1,0:T(8,128)S(1)}, u32[]{:S(2)}, u32[]{:S(2)}) collective-permute-start(f32[128,2048]{1,0:T(8,128)} %green_ref.1), channel_id=1, source_target_pairs={{0,64},{64,0},{1,65},{65,1},{2,66},{66,2},{3,67},{67,3},{4,68},{68... | collective-permute-start | bytes 3145736 | tf_op jit(solution)/shard_map/ppermute | solution.py:18
  3.2 26.5 %collective-permute-start.1 = (f32[128,2048]{1,0:T(8,128)}, f32[128,2048]{1,0:T(8,128)S(1)}, u32[]{:S(2)}, u32[]{:S(2)}) collective-permute-start(f32[128,2048]{1,0:T(8,128)} %green_ref.1), channel_id=1, source_target_pairs={{0,128},{128,0},{1,129},{129,1},{2,130},{130,2},{3,131},{131,3},{4... | collective-permute-start | bytes 3145736 | tf_op jit(solution)/shard_map/ppermute | solution.py:18
  4.2 21.5 %collective-permute-start.2 = (f32[8,4096]{1,0:T(8,128)}, f32[8,4096]{1,0:T(8,128)S(1)}, u32[]{:S(2)}, u32[]{:S(2)}) collective-permute-start(f32[8,4096]{1,0:T(8,128)} %param.5), channel_id=1, source_target_pairs={{0,48},{16,0},{32,16},{48,32},{1,49},{17,1},{33,17},{49,33},{2,50}... | collective-permute-start | bytes 393224 | tf_op jit(solution)/shard_map/ppermute | solution.py:22
  10.3 15.5 %collective-permute-start.3 = (f32[8,4096]{1,0:T(8,128)}, f32[8,4096]{1,0:T(8,128)S(1)}, u32[]{:S(2)}, u32[]{:S(2)}) collective-permute-start(f32[8,4096]{1,0:T(8,128)} %param.5), channel_id=1, source_target_pairs={{0,32},{16,48},{32,0},{48,16},{1,33},{17,49},{33,1},{49,17},{2,34}... | collective-permute-start | bytes 393224 | tf_op jit(solution)/shard_map/ppermute | solution.py:22
  11.2 14.7 %collective-permute-start.4 = (f32[8,4096]{1,0:T(8,128)}, f32[8,4096]{1,0:T(8,128)S(1)}, u32[]{:S(2)}, u32[]{:S(2)}) collective-permute-start(f32[8,4096]{1,0:T(8,128)} %param.5), channel_id=1, source_target_pairs={{0,16},{16,32},{32,48},{48,0},{1,17},{17,33},{33,49},{49,1},{2,18}... | collective-permute-start | bytes 393224 | tf_op jit(solution)/shard_map/ppermute | solution.py:22
  14.5 1.0 copy-start.1
  21.1 12.0 %all-to-all-start = ((f32[8,64,256]{2,1,0:T(8,128)}), f32[8,64,256]{2,1,0:T(8,128)S(1)}, u32[]{:S(2)}, u32[]{:S(2)}) async-start(f32[8,64,256]{2,1,0:T(8,128)} %bitcast.10), calls=%async_computation | async-start | bytes 1048576 | tf_op jit(solution)/shard_map/all_to_all | solution.py:26
  33.2 5.5 %collective-permute-start.5 = (f32[128,2048]{1,0:T(8,128)S(1)}, f32[128,2048]{1,0:T(8,128)S(1)}, u32[]{:S(2)}, u32[]{:S(2)}) collective-permute-start(f32[128,2048]{1,0:T(8,128)S(1)} %collective-permute-done.1.green_x_ref), channel_id=1, source_target_pairs={{0,64},{64,0},{1,65},{65,1},{2,66},{66,2},{3,67},{67,3},{4,68},{68... | collective-permute-start | bytes 3145736 | tf_op jit(solution)/shard_map/ppermute | solution.py:18
  36.4 13.6 %collective-permute-start.6 = (f32[32,4096]{1,0:T(8,128)S(1)}, f32[32,4096]{1,0:T(8,128)S(1)}, u32[]{:S(2)}, u32[]{:S(2)}) collective-permute-start(f32[32,4096]{1,0:T(8,128)S(1)} %constant_dynamic-update-slice_fusion.refs_0_), channel_id=1, source_target_pairs={{0,6},{2,0},{4,2},{6,4},{1,7},{3,1},{5,3},{7,5},{8,14},{10,8},{12,... | collective-permute-start | bytes 1572872 | tf_op jit(solution)/shard_map/ppermute | solution.py:22
  38.7 2.2 %copy-start = (bf16[2,2,256,2048]{3,2,1,0:T(8,128)(2,1)S(1)}, bf16[2,2,256,2048]{3,2,1,0:T(8,128)(2,1)}, u32[]{:S(2)}) copy-start(bf16[2,2,256,2048]{3,2,1,0:T(8,128)(2,1)} %get-tuple-element.19.rows_ref) | copy-start | bytes 12582916
  50.0 24.2 %all-to-all-start.1 = ((f32[8,64,256]{2,1,0:T(8,128)}), f32[8,64,256]{2,1,0:T(8,128)S(1)}, u32[]{:S(2)}, u32[]{:S(2)}) async-start(f32[8,64,256]{2,1,0:T(8,128)} %bitcast.2), calls=%async_computation.1 | async-start | bytes 1048576 | tf_op jit(solution)/shard_map/all_to_all | solution.py:26
  54.0 20.1 %collective-permute-start.7 = (f32[32,4096]{1,0:T(8,128)S(1)}, f32[32,4096]{1,0:T(8,128)S(1)}, u32[]{:S(2)}, u32[]{:S(2)}) collective-permute-start(f32[32,4096]{1,0:T(8,128)S(1)} %constant_dynamic-update-slice_fusion.refs_0_), channel_id=1, source_target_pairs={{0,2},{2,4},{4,6},{6,0},{1,3},{3,5},{5,7},{7,1},{8,10},{10,12},{12... | collective-permute-start | bytes 1572872 | tf_op jit(solution)/shard_map/ppermute | solution.py:22
  74.3 12.9 %collective-permute-start.8 = (f32[32,2048]{1,0:T(8,128)S(1)}, f32[32,2048]{1,0:T(8,128)S(1)}, u32[]{:S(2)}, u32[]{:S(2)}) collective-permute-start(f32[32,2048]{1,0:T(8,128)S(1)} %slice.38), channel_id=1, source_target_pairs={{0,6},{2,0},{4,2},{6,4},{1,7},{3,1},{5,3},{7,5},{8,14},{10,8},{12,... | collective-permute-start | bytes 786440 | tf_op jit(solution)/shard_map/ppermute | solution.py:22
  74.4 12.8 %collective-permute-start.9 = (f32[32,2048]{1,0:T(8,128)S(1)}, f32[32,2048]{1,0:T(8,128)S(1)}, u32[]{:S(2)}, u32[]{:S(2)}) collective-permute-start(f32[32,2048]{1,0:T(8,128)S(1)} %slice.39), channel_id=1, source_target_pairs={{0,2},{2,4},{4,6},{6,0},{1,3},{3,5},{5,7},{7,1},{8,10},{10,12},{12... | collective-permute-start | bytes 786440 | tf_op jit(solution)/shard_map/ppermute | solution.py:22
  87.8 4.7 %collective-permute-start.10 = (f32[8,8,1024]{2,1,0:T(8,128)S(1)}, f32[8,8,1024]{2,1,0:T(8,128)S(1)}, u32[]{:S(2)}, u32[]{:S(2)}) collective-permute-start(f32[8,8,1024]{2,1,0:T(8,128)S(1)} %get-tuple-element.28), channel_id=1, source_target_pairs={{0,64},{64,0},{1,65},{65,1},{2,66},{66,2},{3,67},{67,3},{4,68},{68... | collective-permute-start | bytes 786440 | tf_op jit(solution)/shard_map/ppermute | solution.py:18
